TPU v7x, 128 devices: a whole 4x4x4 slice. The times are simulated.
128 devices in a mesh: row: 8 (over y, core), col: 16 (over z, x).
Axes of the slice: x: 4, y: 4, z: 4, core: 2. Of those that a mesh axis runs over, the one named last changes fastest.
Arguments:
- three_center: bfloat16 [8, 96, 1024, 1024], P('row', 'col'), may hold values from -1 to 1, as said below
- density: bfloat16 [1536, 1536], P('row', 'col'), may hold values from -6 to 6, as said below
- neighbors: int32 [8, 32], P('row'), may hold values from 0 to 47, as said below
- atom_slot: int32 [48], replicated, may hold values from 0 to 47, each once
Outputs:
- exchange: float32 [1536, 1536], P('row', 'col')
Inputs may be any that keep to these rules, and one draw needn't show every extreme that they name: `neighbors`: each row lists 32 different atoms, and every atom of the window is listed in some row. `atom_slot`: each storage position holds exactly one atom. Each matrix three_center[a, p] is symmetric. The density matrix is symmetric.
All inputs are finite; a program needn't handle non-finite values.
Results may differ from a plain program's by a relative error of at most 0.0029.
Values may be sent and summed in bfloat16 or wider, within the bound.
No kernel may reach another device: no remote copies, remote signals or barrier semaphores. Data moves between devices by JAX's collectives and lax.ppermute only.
A program may use at most 256 MiB of HBM per device.

v0:
```python
import jax
import jax.numpy as jnp
from jax import lax
from jax.sharding import PartitionSpec as P


def shards(three_center, density, neighbors, atom_slot):
    nrow = lax.axis_size("row")
    ncol = lax.axis_size("col")
    natoms = atom_slot.shape[0]
    nbhood = neighbors.shape[1]
    width = three_center.shape[2]
    block = width // nbhood
    total = natoms * block
    slots = jnp.take(atom_slot, neighbors[0], axis=0)
    panel = lax.all_gather(density, "row", axis=0, tiled=True)
    whole = lax.all_gather(panel, "col", axis=1, tiled=True)
    chosen = jnp.take(whole.reshape(natoms, block, whole.shape[1]), slots, axis=0)
    rows = chosen.reshape(width, whole.shape[1])
    local_density = jnp.take(rows.reshape(width, natoms, block), slots, axis=1).reshape(
        width, width
    )
    tensor = three_center[0]
    half = jnp.einsum(
        "pij,jk->pik", tensor, local_density, preferred_element_type=jnp.float32
    ).astype(jnp.bfloat16)
    local_exchange = jnp.einsum("pik,plk->il", half, tensor, preferred_element_type=jnp.float32)
    onehot = (slots[:, None] == jnp.arange(natoms, dtype=jnp.int32)[None, :]).astype(jnp.float32)
    blocks = local_exchange.reshape(nbhood, block, nbhood, block)
    onehot_rows = onehot.reshape(nbhood, nrow, natoms // nrow)
    onehot_cols = onehot.reshape(nbhood, ncol, natoms // ncol)
    placed = jnp.einsum(
        "kpa,kxly,lqb->pqaxby", onehot_rows, blocks, onehot_cols, precision=lax.Precision.HIGHEST
    )
    placed = placed.reshape(nrow * ncol * (total // nrow), total // ncol)
    result = lax.psum_scatter(placed, ("row", "col"), scatter_dimension=0, tiled=True)
    return result


def solution(mesh):
    placed = (P("row", "col", None, None), P("row", "col"), P("row", None), P())
    return jax.shard_map(
        shards, mesh=mesh, in_specs=placed, out_specs=P("row", "col"), check_vma=False
    )
```

profile of v0, /device:TPU:65, one launch (start us, length us, event | category | flops | bytes accessed | tf_op | source)
XLA Modules:
  0.0 570.1 jit_solution(5410956695665264040)
XLA Ops:
  6.5 14.3 %all_gather.6 = bf16[1536,96]{1,0:T(8,128)(2,1)S(1)} all-gather(bf16[192,96]{1,0:T(8,128)(2,1)} %param.5), channel_id=1, replica_groups=mesh['row'=8,'col'=16] {'row'}, dimensions={0}, use_global_device_ids=true | all-gather | bytes 331776 | tf_op jit(solution)/shard_map/all_gather | solution.py:16
  20.9 0.9 copy.28
  21.9 0.7 fusion.23
  22.5 0.7 gather_fusion
  23.2 1.2 compare_and_fusion
  24.5 0.1 broadcast_in_dim.37
  24.6 0.6 multiply_add_fusion.1
  25.2 0.6 multiply_add_fusion
  25.8 0.7 fusion.22
  26.4 49.8 %all-gather.2.cloned.1.call-done = bf16[1536,1536]{0,1:T(8,128)(2,1)} async-done(((bf16[1536,96]{0,1:T(8,128)(2,1)}), bf16[1536,1536]{0,1:T(8,128)(2,1)}) %all-gather.2.cloned.1.call-update) | async-done | bytes 4718608 | tf_op jit(solution)/shard_map/all_gather | solution.py:17
  76.3 6.7 %copy.29 = bf16[1536,1536]{1,0:T(8,128)(2,1)} copy(bf16[1536,1536]{0,1:T(8,128)(2,1)} %all-gather.2.cloned.1.call-done) | data formatting | bytes 9437184 | tf_op jit(solution)/shard_map/all_gather | solution.py:17
  83.0 3.1 gather_fusion.1
  86.1 9.8 %gather.19 = bf16[1024,48,32]{2,1,0:T(8,128)(2,1)} reshape(bf16[32,32,1536]{2,1,0:T(8,128)(2,1)S(1)} %gather_fusion.1) | data formatting | bytes 6291456 | tf_op jit(solution)/shard_map/jit(_take)/gather | solution.py:18
  95.9 12.2 %copy.30 = bf16[1024,48,32]{0,2,1:T(8,128)(2,1)S(1)} copy(bf16[1024,48,32]{2,1,0:T(8,128)(2,1)} %gather.19) | data formatting | bytes 6291456 | tf_op jit(solution)/shard_map/jit(_take)/gather | solution.py:18
  108.0 1.9 broadcast_select_fusion
  110.0 2.6 gather_fusion.2
  112.6 0.3 broadcast_select_fusion.1
  112.8 20.4 %fusion.11 = bf16[1024,6,1024]{0,2,1:T(8,128)(2,1)} fusion(bf16[1024,1024,1]{0,1,2:T(8,128)(2,1)S(1)} %bitcast.62, bf16[1,6,1024,1024]{3,2,1,0:T(8,128)(2,1)} %param.4), kind=kOutput, calls=%fused_computation.13 | convolution fusion | flops 12891193344 | bytes 27262976 | tf_op jit(solution)/shard_map/pij,jk->pik/dot_general | solution.py:24
  133.2 65.8 %fusion.5 = f32[32,32,32,32,1]{3,0,4,2,1:T(8,128)} fusion(bf16[32,32,1024,6,1]{2,1,0,3,4:T(8,128)(2,1)} %bitcast.64, bf16[32,32,1024,6]{2,1,0,3:T(8,128)(2,1)} %bitcast.63), kind=kOutput, calls=%fused_computation.6 | convolution fusion | flops 12884901888 | bytes 29360128 | tf_op jit(solution)/shard_map/pik,plk->il/dot_general | solution.py:27
  199.0 18.9 %convolution_bitcast_fusion = f32[32,32,32,8,6,1]{2,3,4,1,0,5:T(8,128)} fusion(f32[32,32,32,32,1]{3,0,4,2,1:T(8,128)} %fusion.5, s32[8,6]{0,1:T(8,128)S(1)} %copy-done.2, s32[32]{0:T(128)S(1)} %copy-done.4), kind=kOutput, calls=%fused_computation.12 | convolution fusion | flops 603981312 | bytes 10486080 | tf_op jit(solution)/shard_map/kpa,kxly,lqb->pqaxby/dot_general | solution.py:32
  217.9 36.8 %fusion.2 = f32[8,16,6,32,3,32]{5,1,4,2,0,3:T(8,128)} fusion(f32[32,32,32,8,6,1]{2,3,4,1,0,5:T(8,128)} %convolution_bitcast_fusion, s32[16,3]{0,1:T(4,128)S(1)} %copy-done.3, s32[32]{0:T(128)S(1)} %copy-done.4), kind=kOutput, calls=%fused_computation.5 | convolution fusion | flops 905971200 | bytes 15728960 | tf_op jit(solution)/shard_map/kpa,kxly,lqb->pqaxby/dot_general | solution.py:32
  254.7 42.5 %copy.53 = f32[8,16,6,32,3,32]{5,4,3,2,1,0:T(4,128)} copy(f32[8,16,6,32,3,32]{5,1,4,2,0,3:T(8,128)} %fusion.2) | data formatting | bytes 18874368
  297.3 47.5 %reshape.193 = f32[24576,96]{1,0:T(8,128)} reshape(f32[8,16,6,32,3,32]{5,4,3,2,1,0:T(4,128)} %copy.53) | data formatting | bytes 18874368
  344.8 218.5 %reduce-scatter.4.cloned.1.call-done = f32[192,96]{1,0:T(8,128)} async-done(((f32[24576,96]{1,0:T(8,128)}), f32[192,96]{1,0:T(8,128)}) %reduce-scatter.4.cloned.1.call-update) | async-done | bytes 73744 | tf_op jit(solution)/shard_map/reduce_scatter | solution.py:36
  (17 shorter events, 0.2 us)
Async XLA Ops:
  6.5 16.0 %copy-start = (s32[48]{0:T(128)S(1)}, s32[48]{0:T(128)}, u32[]{:S(2)}) copy-start(s32[48]{0:T(128)} %param.7) | copy-start | bytes 580
  6.5 69.7 %all-gather.2.cloned.1.call-start = ((), (), s32[]{:S(2)}) async-start(), calls=%async_computation.1 | async-start | bytes 5013504 | tf_op jit(solution)/shard_map/all_gather | solution.py:17
  21.8 541.5 %reduce-scatter.4.cloned.1.call-start = ((), (), s32[]{:S(2)}) async-start(), calls=%async_computation.2 | async-start | bytes 12681216 | tf_op jit(solution)/shard_map/reduce_scatter | solution.py:36
  133.2 65.8 %copy-start.2 = (s32[8,6]{0,1:T(8,128)S(1)}, s32[8,6]{0,1:T(8,128)}, u32[]{:S(2)}) copy-start(s32[8,6]{0,1:T(8,128)} %multiply_add_fusion) | copy-start | bytes 580
  133.2 65.8 %copy-start.4 = (s32[32]{0:T(128)S(1)}, s32[32]{0:T(128)}, u32[]{:S(2)}) copy-start(s32[32]{0:T(128)} %get-tuple-element.6) | copy-start | bytes 388
  199.0 18.9 %copy-start.3 = (s32[16,3]{0,1:T(4,128)S(1)}, s32[16,3]{0,1:T(4,128)}, u32[]{:S(2)}) copy-start(s32[16,3]{0,1:T(4,128)} %multiply_add_fusion.1) | copy-start | bytes 580
  297.2 266.0 %copy-start.1 = (s32[48]{0:T(128)S(1)}, s32[48]{0:T(128)}, u32[]{:S(2)}) copy-start(s32[48]{0:T(128)} %param.7) | copy-start | bytes 580
Sparse Core Ops, SparseCore 0:
  21.9 54.3 all-gather.1
  344.9 218.3 reduce-scatter.3
where the time goes:
time: 576 us; the launch traced here: 570 us
  waiting for transfers between devices  268 us (47%)
  matrix products  142 us (25%)
  local copies, waits for them, and re-layouts  126 us (22%)
  blocking collectives  14.3 us (2%)
  between operations  13.4 us (2%)
  other arithmetic  5.92 us (1%)
    reduce_scatter x1, waiting for transfers between devices, shards(): lax.psum_scatter(placed, ('row', 'col'), scatter_dimension=0, tiled=True)  218 us
    unnamed x12, local copies, waits for them, and re-layouts  90 us
    dot_general x1, matrix products, shards(): jnp.einsum('pik,plk->il', half, tensor, preferred_element_type=jnp.float32)  65.8 us
    dot_general x2, matrix products, shards(): jnp.einsum('kpa,kxly,lqb->pqaxby', onehot_rows, blocks, onehot_cols, prec...  55.7 us
    all_gather x1, waiting for transfers between devices, shards(): whole = lax.all_gather(panel, 'col', axis=1, tiled=True)  49.8 us
    gather x3, local copies, waits for them, and re-layouts, shards(): jnp.take(whole.reshape(natoms, block, whole.shape[1]), slots, axis=0)  25 us
    dot_general x1, matrix products, shards(): jnp.einsum('pij,jk->pik', tensor, local_density, preferred_element_type=j...  20.4 us
    all_gather x1, blocking collectives, shards(): panel = lax.all_gather(density, 'row', axis=0, tiled=True)  14.3 us
  transfers between devices with their start and end apart: 2, of which 2 were waited for; matrix products, arithmetic and copies ran while one was open for 1% of the time, Pallas kernels for 0%

commit v1 on v0

v1 whole, which is shorter than its diff:
```python
import functools

import jax
import jax.numpy as jnp
from jax import lax
from jax.experimental import pallas as pl
from jax.experimental.pallas import tpu as pltpu
from jax.sharding import PartitionSpec as P

BS = 32
KN = 32
NA = 48
LANES = 128
GB = LANES // BS
NG = KN // GB
ND = NG // 2 + 1
WIDTH = KN * BS
KEEP = ND * LANES
MIB = 1 << 20


def params(mib):
    return pltpu.CompilerParams(vmem_limit_bytes=mib * MIB)


def find(slot_of, nb, storage):
    index = jnp.int32(KN)
    for k in range(KN):
        index = jnp.where(slot_of[nb[0, k]] == storage, k, index)
    return index


def select_kernel(ny, ncol, rows, nb, slot_of, p0, p1, p2, p3, out, panel, chosen, turned):
    row = lax.axis_index("row")
    col = lax.axis_index("col")
    y, h = row // 2, row % 2
    for shift, part in enumerate((p0, p1, p2, p3)):
        owner = lax.rem(y - shift + ny, ny)
        for side in range(2):
            at = (2 * owner + (h if side == 0 else 1 - h)) * rows
            panel[pl.ds(pl.multiple_of(at, 32), rows), :96] = part[side * rows : (side + 1) * rows, :]
    for k in range(KN):
        at = pl.multiple_of(slot_of[nb[0, k]] * BS, BS)
        chosen[k * BS : (k + 1) * BS, :] = panel[pl.ds(at, BS), :]
    for i in range(NG):
        tile = chosen[i * LANES : (i + 1) * LANES, :].T
        turned[:, i * LANES : (i + 1) * LANES] = tile
        if i < ND - 1:
            turned[:, (NG + i) * LANES : (NG + i + 1) * LANES] = tile
    per = NA // ncol
    for j in range(per):
        index = find(slot_of, nb, col * per + j)
        group = jnp.where(index < KN, index // GB, 0)
        start = pl.multiple_of(group * LANES, LANES)
        block = turned[j * BS : (j + 1) * BS, pl.ds(start, KEEP)]
        for i in range(ncol):
            out[i, j * BS : (j + 1) * BS, :] = block


def exchange_kernel(nb, slot_of, gathered, tensor, out, local, half, acc):
    step = pl.program_id(0)
    big = 2 * LANES
    tiles = WIDTH // big

    @pl.when(step == 0)
    def _():
        for k in range(KN):
            at = pl.multiple_of(slot_of[nb[0, k]] * BS, BS)
            group = k // GB
            for d in range(ND):
                to = (group + d) % NG
                local[k * BS : (k + 1) * BS, to * LANES : (to + 1) * LANES] = gathered[
                    pl.ds(at, BS), d * LANES : (d + 1) * LANES
                ]
        for group in range(NG):
            for d in range(1, NG // 2):
                to = (group + d) % NG
                local[to * LANES : (to + 1) * LANES, group * LANES : (group + 1) * LANES] = local[
                    group * LANES : (group + 1) * LANES, to * LANES : (to + 1) * LANES
                ].T
        acc[...] = jnp.zeros_like(acc)

    for i in range(tiles):
        half[i * big : (i + 1) * big, :] = jnp.dot(
            local[i * big : (i + 1) * big, :], tensor[0], preferred_element_type=jnp.float32
        ).astype(jnp.bfloat16)
    for i in range(tiles):
        left = tensor[0, i * big : (i + 1) * big, :]
        first = min(tiles - 1, tiles - i)
        acc[i, :, : first * big] += jnp.dot(
            left, half[:, i * big : (i + first) * big], preferred_element_type=jnp.float32
        )
        if first < tiles - 1:
            acc[i, :, first * big :] += jnp.dot(
                left, half[:, : (tiles - 1 - first) * big], preferred_element_type=jnp.float32
            )

    @pl.when(step == pl.num_programs(0) - 1)
    def _():
        ncol = lax.axis_size("col")
        scale = 1.0 + lax.axis_index("col").astype(jnp.float32) / ncol
        out[...] = jnp.zeros_like(out)
        for k in range(KN):
            at = pl.multiple_of(slot_of[nb[0, k]] * BS, BS)
            group = k // GB
            i, odd = group // 2, group % 2
            r = (k % (2 * GB)) * BS
            piece = acc[i, r : r + BS, odd * LANES : odd * LANES + KEEP]
            out[pl.ds(at, BS), :] = (piece * scale).astype(jnp.bfloat16)


def place_kernel(ny, ncol, rows, nb, slot_of, parts, mine, other, total, turned, placed):
    row = lax.axis_index("row")
    col = lax.axis_index("col")
    y, h = row // 2, row % 2
    per = NA // ncol
    sums = parts[0].astype(jnp.float32)
    for i in range(1, ncol):
        sums += parts[i].astype(jnp.float32) * (1.0 / (1.0 + i / ncol))
    total[:96, :] = sums
    for d in range(ND):
        tile = total[:, d * LANES : (d + 1) * LANES].T
        turned[d * LANES : (d + 1) * LANES, :] = tile * 0.5 if d in (0, NG // 2) else tile
    placed[...] = jnp.zeros_like(placed)
    for j in range(per):
        index = find(slot_of, nb, col * per + j)

        @pl.when(index < KN)
        def _():
            group = index // GB
            for d in range(ND):
                to = lax.rem(group + d, NG)
                for b in range(GB):
                    at = pl.multiple_of(slot_of[nb[0, to * GB + b]] * BS, BS)
                    r = d * LANES + b * BS
                    placed[pl.ds(at, BS), j * BS : (j + 1) * BS] = turned[
                        r : r + BS, j * BS : (j + 1) * BS
                    ]

    for shift in range(ny):
        owner = lax.rem(y + shift, ny)
        at = pl.multiple_of((2 * owner + h) * rows, 32)
        mine[shift] = placed[pl.ds(at, rows), :]
        at = pl.multiple_of((2 * owner + 1 - h) * rows, 32)
        other[shift] = placed[pl.ds(at, rows), :]


def mirror_kernel(part, direct, first, second, out):
    b = lax.axis_index("col") % 2
    for side, block in ((b, first), (1 - b, second)):
        at = pl.multiple_of(side * part, 32)
        out[pl.ds(at, part), :] = direct[pl.ds(at, part), :] + block[...].T


VMEM = pl.BlockSpec(memory_space=pltpu.VMEM)
SMEM = pl.BlockSpec(memory_space=pltpu.SMEM)


def shards(three_center, density, neighbors, atom_slot):
    nrow = lax.axis_size("row")
    ncol = lax.axis_size("col")
    ny = nrow // 2
    rows, cols = density.shape
    total = NA * BS
    core = [(i, i ^ 1) for i in range(nrow)]

    def along(k):
        return [(i, (i + 2 * k) % nrow) for i in range(nrow)]

    pair = jnp.concatenate([density, lax.ppermute(density, "row", core)], axis=0)
    others = [lax.ppermute(pair, "row", along(k)) for k in range(1, ny)]
    copies = pl.pallas_call(
        functools.partial(select_kernel, ny, ncol, rows),
        out_shape=jax.ShapeDtypeStruct((ncol, cols, KEEP), jnp.bfloat16),
        in_specs=[SMEM, SMEM] + [VMEM] * 4,
        out_specs=VMEM,
        scratch_shapes=[
            pltpu.VMEM((total, LANES), jnp.bfloat16),
            pltpu.VMEM((WIDTH, LANES), jnp.bfloat16),
            pltpu.VMEM((LANES, WIDTH + KEEP - LANES), jnp.bfloat16),
        ],
        compiler_params=params(24),
        name="select",
    )(neighbors, atom_slot, pair, *others)
    gathered = lax.all_to_all(copies, "col", 0, 0, tiled=True).reshape(total, KEEP)
    tensor = three_center[0]
    nfun = tensor.shape[0]
    sent = pl.pallas_call(
        exchange_kernel,
        out_shape=jax.ShapeDtypeStruct((total, KEEP), jnp.bfloat16),
        grid=(nfun,),
        in_specs=[
            SMEM,
            SMEM,
            pl.BlockSpec((total, KEEP), lambda p: (0, 0)),
            pl.BlockSpec((1, WIDTH, WIDTH), lambda p: (p, 0, 0)),
        ],
        out_specs=pl.BlockSpec((total, KEEP), lambda p: (0, 0)),
        scratch_shapes=[
            pltpu.VMEM((WIDTH, WIDTH), jnp.bfloat16),
            pltpu.VMEM((WIDTH, WIDTH), jnp.bfloat16),
            pltpu.VMEM((4, 2 * LANES, 6 * LANES), jnp.float32),
        ],
        compiler_params=params(48),
        name="exchange",
    )(neighbors, atom_slot, gathered, tensor)
    parts = lax.all_to_all(sent.reshape(ncol, cols, KEEP), "col", 0, 0, tiled=True)
    mine, other = pl.pallas_call(
        functools.partial(place_kernel, ny, ncol, rows),
        out_shape=[jax.ShapeDtypeStruct((ny, rows, cols), jnp.float32)] * 2,
        in_specs=[SMEM, SMEM, VMEM],
        out_specs=[VMEM, VMEM],
        scratch_shapes=[
            pltpu.VMEM((LANES, KEEP), jnp.float32),
            pltpu.VMEM((KEEP, LANES), jnp.float32),
            pltpu.VMEM((total, cols), jnp.float32),
        ],
        compiler_params=params(24),
        name="place",
    )(neighbors, atom_slot, parts)
    chip = mine + lax.ppermute(other, "row", core)
    direct = chip[0]
    for k in range(1, ny):
        direct = direct + lax.ppermute(chip[k], "row", along(k))
    half = rows // 2
    b = lax.axis_index("col") % 2
    same = [(R * ncol + C, (C // 2) * ncol + 2 * R + C % 2) for R in range(nrow) for C in range(ncol)]
    swap = [(R * ncol + C, (C // 2) * ncol + 2 * R + 1 - C % 2) for R in range(nrow) for C in range(ncol)]
    upper, lower = direct[:half], direct[half:]
    first = lax.ppermute(jnp.where(b == 0, upper, lower), ("row", "col"), same)
    second = lax.ppermute(jnp.where(b == 0, lower, upper), ("row", "col"), swap)
    return pl.pallas_call(
        functools.partial(mirror_kernel, half),
        out_shape=jax.ShapeDtypeStruct((rows, cols), jnp.float32),
        in_specs=[VMEM] * 3,
        out_specs=VMEM,
        name="mirror",
    )(direct, first, second)


def solution(mesh):
    placed = (P("row", "col", None, None), P("row", "col"), P("row", None), P())
    return jax.shard_map(
        shards, mesh=mesh, in_specs=placed, out_specs=P("row", "col"), check_vma=False
    )
```

time: 576 us -> 130 us (0.23)
  waiting for transfers between devices: 268 us -> 16.1 us
  matrix products: 142 us -> 0 us
  local copies, waits for them, and re-layouts: 126 us -> 2.77 us
  blocking collectives: 14.3 us -> 57 us
  Pallas kernels: 0 us -> 30.3 us
  starting transfers between devices: 0.04 us -> 23 us
  between operations: 13.4 us -> 0.09 us
  other arithmetic: 5.92 us -> 0.09 us
    reduce_scatter x1 -> x0, waiting for transfers between devices: 218 us -> none  [shards(): lax.psum_scatter(placed, ('row', 'col'), scatter_dimension=0, tiled=True)]
    dot_general x4 -> x0, matrix products: 142 us -> none  [the longest x1 65.8 us: shards(): jnp.einsum('pik,plk->il', half, tensor, preferred_element_type=jnp.float32)]
    unnamed x12 -> x15, local copies, waits for them, and re-layouts: 90 us -> 2.74 us
    all_to_all x0 -> x2, blocking collectives: none -> 57 us  [the longest x1 30.3 us: shards(): lax.all_to_all(copies, 'col', 0, 0, tiled=True).reshape(total, KEEP)]
    all_gather x1 -> x0, waiting for transfers between devices: 49.8 us -> none  [shards(): whole = lax.all_gather(panel, 'col', axis=1, tiled=True)]
    pallas_call x0 -> x4, Pallas kernels: none -> 30.3 us  [the longest x1 26.4 us: shards(): pl.pallas_call(exchange_kernel, out_shape=jax.ShapeDtypeStruct((total, KE...]
    gather x5 -> x0, local copies, waits for them, and re-layouts: 28.3 us -> none  [the longest x3 25 us: shards(): jnp.take(whole.reshape(natoms, block, whole.shape[1]), slots, axis=0)]
    ppermute x0 -> x10, starting transfers between devices: none -> 23 us  [the longest x1 7.01 us: shards(): first = lax.ppermute(jnp.where(b == 0, upper, lower), ('row', 'col'), same)]
  transfers between devices with their start and end apart: 2 -> 10, of which waited for: 2 -> 9; matrix products, arithmetic and copies ran while one was open for 1% -> 1% of each run, Pallas kernels for 0% -> 0%
where the time goes in v1:
time: 130 us; the launch traced here: 129 us
  blocking collectives  57 us (44%)
  Pallas kernels  30.3 us (23%)
  starting transfers between devices  23 us (18%)
  waiting for transfers between devices  16.1 us (12%)
  local copies, waits for them, and re-layouts  2.77 us (2%)
    all_to_all x1, blocking collectives, shards(): lax.all_to_all(copies, 'col', 0, 0, tiled=True).reshape(total, KEEP)  30.3 us
    all_to_all x1, blocking collectives, shards(): lax.all_to_all(sent.reshape(ncol, cols, KEEP), 'col', 0, 0, tiled=True)  26.7 us
    pallas_call x1, Pallas kernels, shards(): pl.pallas_call(exchange_kernel, out_shape=jax.ShapeDtypeStruct((total, KE...  26.4 us
    ppermute x1, starting transfers between devices, shards(): first = lax.ppermute(jnp.where(b == 0, upper, lower), ('row', 'col'), same)  7.01 us
    ppermute x3, starting transfers between devices, shards(): others = [lax.ppermute(pair, 'row', along(k)) for k in range(1, ny)]  5.05 us
    ppermute x1, waiting for transfers between devices, shards(): second = lax.ppermute(jnp.where(b == 0, lower, upper), ('row', 'col'), swap)  4.36 us
    ppermute x3, waiting for transfers between devices, shards(): direct = direct + lax.ppermute(chip[k], 'row', along(k))  4.15 us
    ppermute x1, starting transfers between devices, shards(): chip = mine + lax.ppermute(other, 'row', core)  3.8 us
  transfers between devices with their start and end apart: 10, of which 9 were waited for; matrix products, arithmetic and copies ran while one was open for 1% of the time, Pallas kernels for 0%

profile of v1, /device:TPU:65, one launch (start us, length us, event | category | flops | bytes accessed | tf_op | source)
XLA Modules:
  0.0 129.3 jit_solution(6823096789193471623)
XLA Ops:
  0.0 0.7 collective-permute-start
  0.7 0.8 constant_dynamic-update-slice_fusion.1
  1.8 1.4 %collective-permute-start.1 = (bf16[384,96]{1,0:T(8,128)(2,1)S(1)}, bf16[384,96]{1,0:T(8,128)(2,1)S(1)}, u32[]{:S(2)}, u32[]{:S(2)}) collective-permute-start(bf16[384,96]{1,0:T(8,128)(2,1)S(1)} %constant_dynamic-update-slice_fusion.p0), channel_id=1, source_target_pairs={{0,32},{16,48},{32,64},{48,80},{64,96},{80,112},{96,0},{112,16},{1... | collective-permute-start | bytes 221192 | tf_op jit(solution)/shard_map/ppermute | solution.py:171
  3.1 2.6 %collective-permute-start.2 = (bf16[384,96]{1,0:T(8,128)(2,1)S(1)}, bf16[384,96]{1,0:T(8,128)(2,1)S(1)}, u32[]{:S(2)}, u32[]{:S(2)}) collective-permute-start(bf16[384,96]{1,0:T(8,128)(2,1)S(1)} %constant_dynamic-update-slice_fusion.p0), channel_id=1, source_target_pairs={{0,64},{16,80},{32,96},{48,112},{64,0},{80,16},{96,32},{112,48},{1... | collective-permute-start | bytes 221192 | tf_op jit(solution)/shard_map/ppermute | solution.py:171
  5.8 1.1 collective-permute-start.3
  7.2 3.2 %collective-permute-done.2.p2 = bf16[384,96]{1,0:T(8,128)(2,1)S(1)} collective-permute-done((bf16[384,96]{1,0:T(8,128)(2,1)S(1)}, bf16[384,96]{1,0:T(8,128)(2,1)S(1)}, u32[]{:S(2)}, u32[]{:S(2)}) %collective-permute-start.2) | collective-permute-done | bytes 73760 | tf_op jit(solution)/shard_map/ppermute | solution.py:171
  10.4 0.7 copy-done
  11.7 1.0 select.3
  12.7 30.3 %all_to_all.10 = bf16[16,96,640]{2,1,0:T(8,128)(2,1)S(1)} all-to-all(bf16[16,96,640]{2,1,0:T(8,128)(2,1)S(1)} %select.3), channel_id=1, replica_groups=mesh['row'=8,'col'=16] {'col'}, dimensions={0} | all-to-all | bytes 3932160 | tf_op jit(solution)/shard_map/all_to_all | solution.py:185
  43.0 26.4 %exchange.1 = bf16[1536,640]{1,0:T(8,128)(2,1)S(1)} custom-call(s32[1,32]{1,0:T(1,128)S(1)} %copy-done.1, s32[48]{0:T(128)S(1)} %copy-done.3, bf16[1536,640]{1,0:T(8,128)(2,1)S(1)} %bitcast.17, bf16[6,1024,1024]{2,1,0:T(8,128)(2,1)} %bitcast.19), custom_call_target="tpu_custom_call" | custom-call | tf_op jit(solution)/shard_map/exchange/pallas_call | solution.py:188
  69.4 26.7 %all_to_all.11.parts = bf16[16,96,640]{2,1,0:T(8,128)(2,1)S(1)} all-to-all(bf16[16,96,640]{2,1,0:T(8,128)(2,1)S(1)} %bitcast.18), channel_id=1, replica_groups=mesh['row'=8,'col'=16] {'col'}, dimensions={0} | all-to-all | bytes 3932160 | tf_op jit(solution)/shard_map/all_to_all | solution.py:207
  96.2 1.2 place.1
  97.4 3.8 %collective-permute-start.4 = (f32[4,192,96]{2,1,0:T(8,128)S(1)}, f32[4,192,96]{2,1,0:T(8,128)S(1)}, u32[]{:S(2)}, u32[]{:S(2)}) collective-permute-start(f32[4,192,96]{2,1,0:T(8,128)S(1)} %get-tuple-element.8), channel_id=1, source_target_pairs={{0,16},{16,0},{32,48},{48,32},{64,80},{80,64},{96,112},{112,96},{1... | collective-permute-start | bytes 884744 | tf_op jit(solution)/shard_map/ppermute | solution.py:221
  101.2 1.3 %collective-permute-done.4 = f32[4,192,96]{2,1,0:T(8,128)S(1)} collective-permute-done((f32[4,192,96]{2,1,0:T(8,128)S(1)}, f32[4,192,96]{2,1,0:T(8,128)S(1)}, u32[]{:S(2)}, u32[]{:S(2)}) %collective-permute-start.4) | collective-permute-done | bytes 294944 | tf_op jit(solution)/shard_map/ppermute | solution.py:221
  102.8 2.1 %collective-permute-start.6 = (f32[192,96]{1,0:T(8,128)S(1)}, f32[192,96]{1,0:T(8,128)S(1)}, u32[]{:S(2)}, u32[]{:S(2)}) collective-permute-start(f32[192,96]{1,0:T(8,128)S(1)} %get-tuple-element.11), channel_id=1, source_target_pairs={{0,64},{16,80},{32,96},{48,112},{64,0},{80,16},{96,32},{112,48},{1... | collective-permute-start | bytes 221192 | tf_op jit(solution)/shard_map/ppermute | solution.py:224
  104.9 1.2 collective-permute-start.7
  106.2 2.3 %collective-permute-done.5 = f32[192,96]{1,0:T(8,128)S(1)} collective-permute-done((f32[192,96]{1,0:T(8,128)S(1)}, f32[192,96]{1,0:T(8,128)S(1)}, u32[]{:S(2)}, u32[]{:S(2)}) %collective-permute-start.5) | collective-permute-done | bytes 73760 | tf_op jit(solution)/shard_map/ppermute | solution.py:224
  108.4 1.2 collective-permute-done.6
  109.6 0.7 collective-permute-done.7
  110.4 7.0 %collective-permute-start.8 = (f32[96,96]{1,0:T(8,128)S(1)}, f32[96,96]{1,0:T(8,128)S(1)}, u32[]{:S(2)}, u32[]{:S(2)}) collective-permute-start(f32[96,96]{1,0:T(8,128)S(1)} %get-tuple-element.13), channel_id=1, source_target_pairs={{0,0},{1,1},{2,16},{3,17},{4,32},{5,33},{6,48},{7,49},{8,64},{9,65... | collective-permute-start | bytes 110600 | tf_op jit(solution)/shard_map/ppermute | solution.py:230
  117.4 2.9 %collective-permute-start.9 = (f32[96,96]{1,0:T(8,128)S(1)}, f32[96,96]{1,0:T(8,128)S(1)}, u32[]{:S(2)}, u32[]{:S(2)}) collective-permute-start(f32[96,96]{1,0:T(8,128)S(1)} %get-tuple-element.12), channel_id=1, source_target_pairs={{0,1},{1,0},{2,17},{3,16},{4,33},{5,32},{6,49},{7,48},{8,65},{9,64... | collective-permute-start | bytes 110600 | tf_op jit(solution)/shard_map/ppermute | solution.py:231
  120.3 2.4 %collective-permute-done.8.first = f32[96,96]{1,0:T(8,128)S(1)} collective-permute-done((f32[96,96]{1,0:T(8,128)S(1)}, f32[96,96]{1,0:T(8,128)S(1)}, u32[]{:S(2)}, u32[]{:S(2)}) %collective-permute-start.8) | collective-permute-done | bytes 36896 | tf_op jit(solution)/shard_map/ppermute | solution.py:230
  122.7 4.4 %collective-permute-done.9.second = f32[96,96]{1,0:T(8,128)S(1)} collective-permute-done((f32[96,96]{1,0:T(8,128)S(1)}, f32[96,96]{1,0:T(8,128)S(1)}, u32[]{:S(2)}, u32[]{:S(2)}) %collective-permute-start.9) | collective-permute-done | bytes 36896 | tf_op jit(solution)/shard_map/ppermute | solution.py:231
  127.6 1.7 %mirror.1 = f32[192,96]{1,0:T(8,128)} custom-call(f32[192,96]{1,0:T(8,128)} %copy-done.4, f32[96,96]{1,0:T(8,128)} %copy-done.5, f32[96,96]{1,0:T(8,128)} %copy-done.6), custom_call_target="tpu_custom_call" | custom-call | tf_op jit(solution)/shard_map/mirror/pallas_call | solution.py:232
  (22 shorter events, 2.2 us)
Async XLA Ops:
  0.0 1.8 %collective-permute-start = (bf16[192,96]{1,0:T(8,128)(2,1)}, bf16[192,96]{1,0:T(8,128)(2,1)S(1)}, u32[]{:S(2)}, u32[]{:S(2)}) collective-permute-start(bf16[192,96]{1,0:T(8,128)(2,1)} %param.5), channel_id=1, source_target_pairs={{0,16},{16,0},{32,48},{48,32},{64,80},{80,64},{96,112},{112,96},{1... | collective-permute-start | bytes 110600 | tf_op jit(solution)/shard_map/ppermute | solution.py:170
  1.8 5.4 %collective-permute-start.1 = (bf16[384,96]{1,0:T(8,128)(2,1)S(1)}, bf16[384,96]{1,0:T(8,128)(2,1)S(1)}, u32[]{:S(2)}, u32[]{:S(2)}) collective-permute-start(bf16[384,96]{1,0:T(8,128)(2,1)S(1)} %constant_dynamic-update-slice_fusion.p0), channel_id=1, source_target_pairs={{0,32},{16,48},{32,64},{48,80},{64,96},{80,112},{96,0},{112,16},{1... | collective-permute-start | bytes 221192 | tf_op jit(solution)/shard_map/ppermute | solution.py:171
  3.1 7.3 %collective-permute-start.2 = (bf16[384,96]{1,0:T(8,128)(2,1)S(1)}, bf16[384,96]{1,0:T(8,128)(2,1)S(1)}, u32[]{:S(2)}, u32[]{:S(2)}) collective-permute-start(bf16[384,96]{1,0:T(8,128)(2,1)S(1)} %constant_dynamic-update-slice_fusion.p0), channel_id=1, source_target_pairs={{0,64},{16,80},{32,96},{48,112},{64,0},{80,16},{96,32},{112,48},{1... | collective-permute-start | bytes 221192 | tf_op jit(solution)/shard_map/ppermute | solution.py:171
  5.8 4.7 %collective-permute-start.3 = (bf16[384,96]{1,0:T(8,128)(2,1)S(1)}, bf16[384,96]{1,0:T(8,128)(2,1)S(1)}, u32[]{:S(2)}, u32[]{:S(2)}) collective-permute-start(bf16[384,96]{1,0:T(8,128)(2,1)S(1)} %constant_dynamic-update-slice_fusion.p0), channel_id=1, source_target_pairs={{0,96},{16,112},{32,0},{48,16},{64,32},{80,48},{96,64},{112,80},{1... | collective-permute-start | bytes 221192 | tf_op jit(solution)/shard_map/ppermute | solution.py:171
  10.4 0.7 copy-start
  11.1 0.7 copy-start.2
  12.7 30.3 %copy-start.1 = (s32[1,32]{1,0:T(1,128)S(1)}, s32[1,32]{1,0:T(1,128)}, u32[]{:S(2)}) copy-start(s32[1,32]{1,0:T(1,128)} %nb.5) | copy-start | bytes 388
  12.7 30.3 %copy-start.3 = (s32[48]{0:T(128)S(1)}, s32[48]{0:T(128)}, u32[]{:S(2)}) copy-start(s32[48]{0:T(128)} %slot_of.5) | copy-start | bytes 580
  97.4 5.2 %collective-permute-start.4 = (f32[4,192,96]{2,1,0:T(8,128)S(1)}, f32[4,192,96]{2,1,0:T(8,128)S(1)}, u32[]{:S(2)}, u32[]{:S(2)}) collective-permute-start(f32[4,192,96]{2,1,0:T(8,128)S(1)} %get-tuple-element.8), channel_id=1, source_target_pairs={{0,16},{16,0},{32,48},{48,32},{64,80},{80,64},{96,112},{112,96},{1... | collective-permute-start | bytes 884744 | tf_op jit(solution)/shard_map/ppermute | solution.py:221
  102.7 5.8 %collective-permute-start.5 = (f32[192,96]{1,0:T(8,128)S(1)}, f32[192,96]{1,0:T(8,128)S(1)}, u32[]{:S(2)}, u32[]{:S(2)}) collective-permute-start(f32[192,96]{1,0:T(8,128)S(1)} %get-tuple-element.9), channel_id=1, source_target_pairs={{0,32},{16,48},{32,64},{48,80},{64,96},{80,112},{96,0},{112,16},{1... | collective-permute-start | bytes 221192 | tf_op jit(solution)/shard_map/ppermute | solution.py:224
  102.8 6.8 %collective-permute-start.6 = (f32[192,96]{1,0:T(8,128)S(1)}, f32[192,96]{1,0:T(8,128)S(1)}, u32[]{:S(2)}, u32[]{:S(2)}) collective-permute-start(f32[192,96]{1,0:T(8,128)S(1)} %get-tuple-element.11), channel_id=1, source_target_pairs={{0,64},{16,80},{32,96},{48,112},{64,0},{80,16},{96,32},{112,48},{1... | collective-permute-start | bytes 221192 | tf_op jit(solution)/shard_map/ppermute | solution.py:224
  104.9 5.4 %collective-permute-start.7 = (f32[192,96]{1,0:T(8,128)S(1)}, f32[192,96]{1,0:T(8,128)S(1)}, u32[]{:S(2)}, u32[]{:S(2)}) collective-permute-start(f32[192,96]{1,0:T(8,128)S(1)} %get-tuple-element.10), channel_id=1, source_target_pairs={{0,96},{16,112},{32,0},{48,16},{64,32},{80,48},{96,64},{112,80},{1... | collective-permute-start | bytes 221192 | tf_op jit(solution)/shard_map/ppermute | solution.py:224
  110.3 16.7 %copy-start.4 = (f32[192,96]{1,0:T(8,128)}, f32[192,96]{1,0:T(8,128)S(1)}, u32[]{:S(2)}) copy-start(f32[192,96]{1,0:T(8,128)S(1)} %fusion.2.direct) | copy-start | bytes 221188
  110.4 12.3 %collective-permute-start.8 = (f32[96,96]{1,0:T(8,128)S(1)}, f32[96,96]{1,0:T(8,128)S(1)}, u32[]{:S(2)}, u32[]{:S(2)}) collective-permute-start(f32[96,96]{1,0:T(8,128)S(1)} %get-tuple-element.13), channel_id=1, source_target_pairs={{0,0},{1,1},{2,16},{3,17},{4,32},{5,33},{6,48},{7,49},{8,64},{9,65... | collective-permute-start | bytes 110600 | tf_op jit(solution)/shard_map/ppermute | solution.py:230
  117.4 9.7 %collective-permute-start.9 = (f32[96,96]{1,0:T(8,128)S(1)}, f32[96,96]{1,0:T(8,128)S(1)}, u32[]{:S(2)}, u32[]{:S(2)}) collective-permute-start(f32[96,96]{1,0:T(8,128)S(1)} %get-tuple-element.12), channel_id=1, source_target_pairs={{0,1},{1,0},{2,17},{3,16},{4,33},{5,32},{6,49},{7,48},{8,65},{9,64... | collective-permute-start | bytes 110600 | tf_op jit(solution)/shard_map/ppermute | solution.py:231
  122.7 4.4 %copy-start.5 = (f32[96,96]{1,0:T(8,128)}, f32[96,96]{1,0:T(8,128)S(1)}, u32[]{:S(2)}) copy-start(f32[96,96]{1,0:T(8,128)S(1)} %collective-permute-done.8.first) | copy-start | bytes 110596
  127.0 0.6 copy-start.6

commit v2 on v1

--- a/solution.py
+++ b/solution.py
@@ -1,4 +1,5 @@
 import functools
+import math
 
 import jax
 import jax.numpy as jnp
@@ -30,18 +31,29 @@
     return index
 
 
-def select_kernel(ny, ncol, rows, nb, slot_of, p0, p1, p2, p3, out, panel, chosen, turned):
+def select_kernel(ny, ncol, rows, nb, slot_of, p0, p1, p2, p3, out, panel, chosen, turned, sem):
     row = lax.axis_index("row")
     col = lax.axis_index("col")
     y, h = row // 2, row % 2
+    copies = []
     for shift, part in enumerate((p0, p1, p2, p3)):
         owner = lax.rem(y - shift + ny, ny)
         for side in range(2):
-            at = (2 * owner + (h if side == 0 else 1 - h)) * rows
-            panel[pl.ds(pl.multiple_of(at, 32), rows), :96] = part[side * rows : (side + 1) * rows, :]
+            at = pl.multiple_of((2 * owner + (h if side == 0 else 1 - h)) * rows, 32)
+            copies.append(
+                pltpu.make_async_copy(
+                    part.at[pl.ds(side * rows, rows), :],
+                    panel.at[pl.ds(at, rows), :],
+                    sem.at[2 * shift + side],
+                )
+            )
+    for copy in copies:
+        copy.start()
+    for copy in copies:
+        copy.wait()
     for k in range(KN):
         at = pl.multiple_of(slot_of[nb[0, k]] * BS, BS)
-        chosen[k * BS : (k + 1) * BS, :] = panel[pl.ds(at, BS), :]
+        chosen[k * BS : (k + 1) * BS, :96] = panel[pl.ds(at, BS), :]
     for i in range(NG):
         tile = chosen[i * LANES : (i + 1) * LANES, :].T
         turned[:, i * LANES : (i + 1) * LANES] = tile
@@ -52,18 +64,25 @@
         index = find(slot_of, nb, col * per + j)
         group = jnp.where(index < KN, index // GB, 0)
         start = pl.multiple_of(group * LANES, LANES)
-        block = turned[j * BS : (j + 1) * BS, pl.ds(start, KEEP)]
-        for i in range(ncol):
-            out[i, j * BS : (j + 1) * BS, :] = block
-
-
-def exchange_kernel(nb, slot_of, gathered, tensor, out, local, half, acc):
+        out[j * BS : (j + 1) * BS, :] = turned[j * BS : (j + 1) * BS, pl.ds(start, KEEP)]
+
+
+def exchange_kernel(side, q0, q1, q2, q3, nb, slot_of, tensor, out, gathered, local, half, acc):
     step = pl.program_id(0)
     big = 2 * LANES
     tiles = WIDTH // big
 
     @pl.when(step == 0)
     def _():
+        h = lax.axis_index("row") % 2
+        z, x = lax.axis_index("col") // side, lax.axis_index("col") % side
+        cols = gathered.shape[0] // side**2
+        for j, part in enumerate((q0, q1, q2, q3)):
+            for k in range(side):
+                dz, dx = jnp.where(h == 0, j, k), jnp.where(h == 0, k, j)
+                owner = lax.rem(z - dz + side, side) * side + lax.rem(x - dx + side, side)
+                at = pl.multiple_of(owner * cols, 32)
+                gathered[pl.ds(at, cols), :] = part[k * cols : (k + 1) * cols, :]
         for k in range(KN):
             at = pl.multiple_of(slot_of[nb[0, k]] * BS, BS)
             group = k // GB
@@ -154,6 +173,7 @@
 
 VMEM = pl.BlockSpec(memory_space=pltpu.VMEM)
 SMEM = pl.BlockSpec(memory_space=pltpu.SMEM)
+ANY = pl.BlockSpec(memory_space=pl.ANY)
 
 
 def shards(three_center, density, neighbors, atom_slot):
@@ -169,41 +189,60 @@
 
     pair = jnp.concatenate([density, lax.ppermute(density, "row", core)], axis=0)
     others = [lax.ppermute(pair, "row", along(k)) for k in range(1, ny)]
-    copies = pl.pallas_call(
+    block = pl.pallas_call(
         functools.partial(select_kernel, ny, ncol, rows),
-        out_shape=jax.ShapeDtypeStruct((ncol, cols, KEEP), jnp.bfloat16),
-        in_specs=[SMEM, SMEM] + [VMEM] * 4,
+        out_shape=jax.ShapeDtypeStruct((cols, KEEP), jnp.bfloat16),
+        in_specs=[SMEM, SMEM] + [ANY] * 4,
         out_specs=VMEM,
         scratch_shapes=[
-            pltpu.VMEM((total, LANES), jnp.bfloat16),
+            pltpu.VMEM((total, cols), jnp.bfloat16),
             pltpu.VMEM((WIDTH, LANES), jnp.bfloat16),
             pltpu.VMEM((LANES, WIDTH + KEEP - LANES), jnp.bfloat16),
-        ],
-        compiler_params=params(24),
+            pltpu.SemaphoreType.DMA((2 * ny,)),
+        ],
+        compiler_params=params(12),
         name="select",
     )(neighbors, atom_slot, pair, *others)
-    gathered = lax.all_to_all(copies, "col", 0, 0, tiled=True).reshape(total, KEEP)
+    side = math.isqrt(ncol)
+
+    def stage(k, first):
+        pairs = []
+        for r in range(nrow):
+            for c in range(ncol):
+                z, x = divmod(c, side)
+                if (r % 2 == 0) == first:
+                    x = (x + k) % side
+                else:
+                    z = (z + k) % side
+                pairs.append((r * ncol + c, r * ncol + z * side + x))
+        return pairs
+
+    both = ("row", "col")
+    line = [block] + [lax.ppermute(block, both, stage(k, True)) for k in range(1, side)]
+    line = jnp.concatenate(line, axis=0)
+    plane = [line] + [lax.ppermute(line, both, stage(k, False)) for k in range(1, side)]
     tensor = three_center[0]
     nfun = tensor.shape[0]
     sent = pl.pallas_call(
-        exchange_kernel,
+        functools.partial(exchange_kernel, side),
         out_shape=jax.ShapeDtypeStruct((total, KEEP), jnp.bfloat16),
         grid=(nfun,),
-        in_specs=[
+        in_specs=[pl.BlockSpec(line.shape, lambda p: (0, 0))] * side
+        + [
             SMEM,
             SMEM,
-            pl.BlockSpec((total, KEEP), lambda p: (0, 0)),
             pl.BlockSpec((1, WIDTH, WIDTH), lambda p: (p, 0, 0)),
         ],
         out_specs=pl.BlockSpec((total, KEEP), lambda p: (0, 0)),
         scratch_shapes=[
+            pltpu.VMEM((total, KEEP), jnp.bfloat16),
             pltpu.VMEM((WIDTH, WIDTH), jnp.bfloat16),
             pltpu.VMEM((WIDTH, WIDTH), jnp.bfloat16),
             pltpu.VMEM((4, 2 * LANES, 6 * LANES), jnp.float32),
         ],
         compiler_params=params(48),
         name="exchange",
-    )(neighbors, atom_slot, gathered, tensor)
+    )(*plane, neighbors, atom_slot, tensor)
     parts = lax.all_to_all(sent.reshape(ncol, cols, KEEP), "col", 0, 0, tiled=True)
     mine, other = pl.pallas_call(
         functools.partial(place_kernel, ny, ncol, rows),
@@ -215,7 +254,7 @@
             pltpu.VMEM((KEEP, LANES), jnp.float32),
             pltpu.VMEM((total, cols), jnp.float32),
         ],
-        compiler_params=params(24),
+        compiler_params=params(12),
         name="place",
     )(neighbors, atom_slot, parts)
     chip = mine + lax.ppermute(other, "row", core)
@@ -234,6 +273,7 @@
         out_shape=jax.ShapeDtypeStruct((rows, cols), jnp.float32),
         in_specs=[VMEM] * 3,
         out_specs=VMEM,
+        compiler_params=params(12),
         name="mirror",
     )(direct, first, second)
 

time: 130 us -> 125 us (0.962)
  blocking collectives: 57 us -> 27.3 us
  waiting for transfers between devices: 16.1 us -> 31 us
  starting transfers between devices: 23 us -> 32.4 us
    all_to_all x1 -> x0, blocking collectives: 30.3 us -> none  [shards(): lax.all_to_all(copies, 'col', 0, 0, tiled=True).reshape(total, KEEP)]
    ppermute x0 -> x6, waiting for transfers between devices: none -> 14.6 us  [the longest x3 10.3 us: shards(): lax.ppermute(line, both, stage(k, False))]
    ppermute x0 -> x6, starting transfers between devices: none -> 7.87 us  [the longest x3 5.18 us: shards(): lax.ppermute(line, both, stage(k, False))]
    unnamed x15 -> x9, local copies, waits for them, and re-layouts: 2.74 us -> 3.42 us
  transfers between devices with their start and end apart: 10 -> 16, of which waited for: 9 -> 13; matrix products, arithmetic and copies ran while one was open for 1% -> 1% of each run, Pallas kernels for 0% -> 0%
where the time goes in v2:
time: 125 us; the launch traced here: 124 us
  starting transfers between devices  32.4 us (26%)
  waiting for transfers between devices  31 us (25%)
  Pallas kernels  30 us (24%)
  blocking collectives  27.3 us (22%)
  local copies, waits for them, and re-layouts  3.45 us (3%)
    all_to_all x1, blocking collectives, shards(): lax.all_to_all(sent.reshape(ncol, cols, KEEP), 'col', 0, 0, tiled=True)  27.3 us
    pallas_call x1, Pallas kernels, shards(): pl.pallas_call(functools.partial(exchange_kernel, side), out_shape=jax.Sh...  26.6 us
    ppermute x3, waiting for transfers between devices, shards(): lax.ppermute(line, both, stage(k, False))  10.3 us
    ppermute x1, starting transfers between devices, shards(): first = lax.ppermute(jnp.where(b == 0, upper, lower), ('row', 'col'), same)  7.24 us
    ppermute x1, waiting for transfers between devices, shards(): second = lax.ppermute(jnp.where(b == 0, lower, upper), ('row', 'col'), swap)  5.38 us
    ppermute x3, starting transfers between devices, shards(): lax.ppermute(line, both, stage(k, False))  5.18 us
    ppermute x3, starting transfers between devices, shards(): others = [lax.ppermute(pair, 'row', along(k)) for k in range(1, ny)]  5.05 us
    ppermute x1, starting transfers between devices, shards(): chip = mine + lax.ppermute(other, 'row', core)  5.03 us
  transfers between devices with their start and end apart: 16, of which 13 were waited for; matrix products, arithmetic and copies ran while one was open for 1% of the time, Pallas kernels for 0%

profile of v2, /device:TPU:65, one launch (start us, length us, event | category | flops | bytes accessed | tf_op | source)
XLA Modules:
  0.0 124.5 jit_solution(10055040844401862440)
XLA Ops:
  1.8 1.4 %collective-permute-start.1 = (bf16[384,96]{1,0:T(8,128)(2,1)S(1)}, bf16[384,96]{1,0:T(8,128)(2,1)S(1)}, u32[]{:S(2)}, u32[]{:S(2)}) collective-permute-start(bf16[384,96]{1,0:T(8,128)(2,1)S(1)} %constant_dynamic-update-slice_fusion.p0), channel_id=1, source_target_pairs={{0,32},{16,48},{32,64},{48,80},{64,96},{80,112},{96,0},{112,16},{1... | collective-permute-start | bytes 221192 | tf_op jit(solution)/shard_map/ppermute | solution.py:191
  3.1 2.6 %collective-permute-start.2 = (bf16[384,96]{1,0:T(8,128)(2,1)S(1)}, bf16[384,96]{1,0:T(8,128)(2,1)S(1)}, u32[]{:S(2)}, u32[]{:S(2)}) collective-permute-start(bf16[384,96]{1,0:T(8,128)(2,1)S(1)} %constant_dynamic-update-slice_fusion.p0), channel_id=1, source_target_pairs={{0,64},{16,80},{32,96},{48,112},{64,0},{80,16},{96,32},{112,48},{1... | collective-permute-start | bytes 221192 | tf_op jit(solution)/shard_map/ppermute | solution.py:191
  7.2 3.2 %collective-permute-done.2.p2 = bf16[384,96]{1,0:T(8,128)(2,1)S(1)} collective-permute-done((bf16[384,96]{1,0:T(8,128)(2,1)S(1)}, bf16[384,96]{1,0:T(8,128)(2,1)S(1)}, u32[]{:S(2)}, u32[]{:S(2)}) %collective-permute-start.2) | collective-permute-done | bytes 73760 | tf_op jit(solution)/shard_map/ppermute | solution.py:191
  11.7 1.4 %select.3 = bf16[96,640]{1,0:T(8,128)(2,1)S(1)} custom-call(s32[1,32]{1,0:T(1,128)S(1)} %copy-done, s32[48]{0:T(128)S(1)} %copy-done.2, bf16[384,96]{1,0:T(8,128)(2,1)S(1)} %constant_dynamic-update-slice_fusion.p0, bf16[384,96]{1,0:T(8,128)(2,1)S(1)} %collective-permute-done.1.p1, bf16[384,96]{1,0:T(8,128)(2,1)S(1)} %collective-permute-done.2.p2, ...), custom_call_target="tpu_custom_call" | custom-call | tf_op jit(solution)/shard_map/select/pallas_call | solution.py:192
  13.2 1.4 %collective-permute-start.4 = (bf16[96,640]{1,0:T(8,128)(2,1)S(1)}, bf16[96,640]{1,0:T(8,128)(2,1)S(1)}, u32[]{:S(2)}, u32[]{:S(2)}) collective-permute-start(bf16[96,640]{1,0:T(8,128)(2,1)S(1)} %select.3), channel_id=1, source_target_pairs={{0,1},{1,2},{2,3},{3,0},{4,5},{5,6},{6,7},{7,4},{8,9},{9,10},{10,1... | collective-permute-start | bytes 368648 | tf_op jit(solution)/shard_map/ppermute | solution.py:221
  14.6 1.3 %collective-permute-start.6 = (bf16[96,640]{1,0:T(8,128)(2,1)S(1)}, bf16[96,640]{1,0:T(8,128)(2,1)S(1)}, u32[]{:S(2)}, u32[]{:S(2)}) collective-permute-start(bf16[96,640]{1,0:T(8,128)(2,1)S(1)} %select.3), channel_id=1, source_target_pairs={{0,3},{1,0},{2,1},{3,2},{4,7},{5,4},{6,5},{7,6},{8,11},{9,8},{10,9... | collective-permute-start | bytes 368648 | tf_op jit(solution)/shard_map/ppermute | solution.py:221
  17.0 3.1 %collective-permute-done.5 = bf16[96,640]{1,0:T(8,128)(2,1)S(1)} collective-permute-done((bf16[96,640]{1,0:T(8,128)(2,1)S(1)}, bf16[96,640]{1,0:T(8,128)(2,1)S(1)}, u32[]{:S(2)}, u32[]{:S(2)}) %collective-permute-start.5) | collective-permute-done | bytes 122912 | tf_op jit(solution)/shard_map/ppermute | solution.py:221
  20.2 1.6 %collective-permute-start.7 = (bf16[384,640]{1,0:T(8,128)(2,1)S(1)}, bf16[384,640]{1,0:T(8,128)(2,1)S(1)}, u32[]{:S(2)}, u32[]{:S(2)}) collective-permute-start(bf16[384,640]{1,0:T(8,128)(2,1)S(1)} %pad_maximum_fusion.q0), channel_id=1, source_target_pairs={{0,4},{1,5},{2,6},{3,7},{4,8},{5,9},{6,10},{7,11},{8,12},{9,13},{1... | collective-permute-start | bytes 1474568 | tf_op jit(solution)/shard_map/ppermute | solution.py:223
  21.7 2.5 %collective-permute-start.8 = (bf16[384,640]{1,0:T(8,128)(2,1)S(1)}, bf16[384,640]{1,0:T(8,128)(2,1)S(1)}, u32[]{:S(2)}, u32[]{:S(2)}) collective-permute-start(bf16[384,640]{1,0:T(8,128)(2,1)S(1)} %pad_maximum_fusion.q0), channel_id=1, source_target_pairs={{0,8},{1,9},{2,10},{3,11},{4,12},{5,13},{6,14},{7,15},{8,0},{9,1},... | collective-permute-start | bytes 1474568 | tf_op jit(solution)/shard_map/ppermute | solution.py:223
  25.3 3.9 %collective-permute-done.7.q1 = bf16[384,640]{1,0:T(8,128)(2,1)S(1)} collective-permute-done((bf16[384,640]{1,0:T(8,128)(2,1)S(1)}, bf16[384,640]{1,0:T(8,128)(2,1)S(1)}, u32[]{:S(2)}, u32[]{:S(2)}) %collective-permute-start.7) | collective-permute-done | bytes 491552 | tf_op jit(solution)/shard_map/ppermute | solution.py:223
  29.2 6.4 %collective-permute-done.8.q2 = bf16[384,640]{1,0:T(8,128)(2,1)S(1)} collective-permute-done((bf16[384,640]{1,0:T(8,128)(2,1)S(1)}, bf16[384,640]{1,0:T(8,128)(2,1)S(1)}, u32[]{:S(2)}, u32[]{:S(2)}) %collective-permute-start.8) | collective-permute-done | bytes 491552 | tf_op jit(solution)/shard_map/ppermute | solution.py:223
  37.0 26.6 %exchange.1 = bf16[1536,640]{1,0:T(8,128)(2,1)S(1)} custom-call(bf16[384,640]{1,0:T(8,128)(2,1)S(1)} %pad_maximum_fusion.q0, bf16[384,640]{1,0:T(8,128)(2,1)S(1)} %collective-permute-done.7.q1, bf16[384,640]{1,0:T(8,128)(2,1)S(1)} %collective-permute-done.8.q2, bf16[384,640]{1,0:T(8,128)(2,1)S(1)} %collective-permute-done.9.q3, s32[1,32]{1,0:T(1,128)S(1)} %copy-done.1, ...), custom_call_target="tpu_custom_call" | custom-call | tf_op jit(solution)/shard_map/exchange/pallas_call | solution.py:226
  63.6 27.3 %all_to_all.5.parts = bf16[16,96,640]{2,1,0:T(8,128)(2,1)S(1)} all-to-all(bf16[16,96,640]{2,1,0:T(8,128)(2,1)S(1)} %bitcast.16), channel_id=1, replica_groups=mesh['row'=8,'col'=16] {'col'}, dimensions={0} | all-to-all | bytes 3932160 | tf_op jit(solution)/shard_map/all_to_all | solution.py:246
  90.9 1.2 place.1
  92.2 5.0 %collective-permute-start.10 = (f32[4,192,96]{2,1,0:T(8,128)S(1)}, f32[4,192,96]{2,1,0:T(8,128)S(1)}, u32[]{:S(2)}, u32[]{:S(2)}) collective-permute-start(f32[4,192,96]{2,1,0:T(8,128)S(1)} %get-tuple-element.8), channel_id=1, source_target_pairs={{0,16},{16,0},{32,48},{48,32},{64,80},{80,64},{96,112},{112,96},{1... | collective-permute-start | bytes 884744 | tf_op jit(solution)/shard_map/ppermute | solution.py:260
  97.2 1.3 %collective-permute-done.10 = f32[4,192,96]{2,1,0:T(8,128)S(1)} collective-permute-done((f32[4,192,96]{2,1,0:T(8,128)S(1)}, f32[4,192,96]{2,1,0:T(8,128)S(1)}, u32[]{:S(2)}, u32[]{:S(2)}) %collective-permute-start.10) | collective-permute-done | bytes 294944 | tf_op jit(solution)/shard_map/ppermute | solution.py:260
  99.3 2.1 %collective-permute-start.12 = (f32[192,96]{1,0:T(8,128)S(1)}, f32[192,96]{1,0:T(8,128)S(1)}, u32[]{:S(2)}, u32[]{:S(2)}) collective-permute-start(f32[192,96]{1,0:T(8,128)S(1)} %get-tuple-element.11), channel_id=1, source_target_pairs={{0,64},{16,80},{32,96},{48,112},{64,0},{80,16},{96,32},{112,48},{1... | collective-permute-start | bytes 221192 | tf_op jit(solution)/shard_map/ppermute | solution.py:263
  101.5 1.3 %collective-permute-start.13 = (f32[192,96]{1,0:T(8,128)S(1)}, f32[192,96]{1,0:T(8,128)S(1)}, u32[]{:S(2)}, u32[]{:S(2)}) collective-permute-start(f32[192,96]{1,0:T(8,128)S(1)} %get-tuple-element.10), channel_id=1, source_target_pairs={{0,96},{16,112},{32,0},{48,16},{64,32},{80,48},{96,64},{112,80},{1... | collective-permute-start | bytes 221192 | tf_op jit(solution)/shard_map/ppermute | solution.py:263
  102.7 1.2 collective-permute-done.11
  103.9 2.2 %collective-permute-done.12 = f32[192,96]{1,0:T(8,128)S(1)} collective-permute-done((f32[192,96]{1,0:T(8,128)S(1)}, f32[192,96]{1,0:T(8,128)S(1)}, u32[]{:S(2)}, u32[]{:S(2)}) %collective-permute-start.12) | collective-permute-done | bytes 73760 | tf_op jit(solution)/shard_map/ppermute | solution.py:263
  106.3 7.2 %collective-permute-start.14 = (f32[96,96]{1,0:T(8,128)S(1)}, f32[96,96]{1,0:T(8,128)S(1)}, u32[]{:S(2)}, u32[]{:S(2)}) collective-permute-start(f32[96,96]{1,0:T(8,128)S(1)} %get-tuple-element.13), channel_id=1, source_target_pairs={{0,0},{1,1},{2,16},{3,17},{4,32},{5,33},{6,48},{7,49},{8,64},{9,65... | collective-permute-start | bytes 110600 | tf_op jit(solution)/shard_map/ppermute | solution.py:269
  113.6 2.5 %collective-permute-start.15 = (f32[96,96]{1,0:T(8,128)S(1)}, f32[96,96]{1,0:T(8,128)S(1)}, u32[]{:S(2)}, u32[]{:S(2)}) collective-permute-start(f32[96,96]{1,0:T(8,128)S(1)} %get-tuple-element.12), channel_id=1, source_target_pairs={{0,1},{1,0},{2,17},{3,16},{4,33},{5,32},{6,49},{7,48},{8,65},{9,64... | collective-permute-start | bytes 110600 | tf_op jit(solution)/shard_map/ppermute | solution.py:270
  116.1 2.3 %collective-permute-done.14.first = f32[96,96]{1,0:T(8,128)S(1)} collective-permute-done((f32[96,96]{1,0:T(8,128)S(1)}, f32[96,96]{1,0:T(8,128)S(1)}, u32[]{:S(2)}, u32[]{:S(2)}) %collective-permute-start.14) | collective-permute-done | bytes 36896 | tf_op jit(solution)/shard_map/ppermute | solution.py:269
  118.3 5.4 %collective-permute-done.15.second = f32[96,96]{1,0:T(8,128)S(1)} collective-permute-done((f32[96,96]{1,0:T(8,128)S(1)}, f32[96,96]{1,0:T(8,128)S(1)}, u32[]{:S(2)}, u32[]{:S(2)}) %collective-permute-start.15) | collective-permute-done | bytes 36896 | tf_op jit(solution)/shard_map/ppermute | solution.py:270
  (28 shorter events, 9.9 us)
Async XLA Ops:
  0.0 1.8 %collective-permute-start = (bf16[192,96]{1,0:T(8,128)(2,1)}, bf16[192,96]{1,0:T(8,128)(2,1)S(1)}, u32[]{:S(2)}, u32[]{:S(2)}) collective-permute-start(bf16[192,96]{1,0:T(8,128)(2,1)} %param.5), channel_id=1, source_target_pairs={{0,16},{16,0},{32,48},{48,32},{64,80},{80,64},{96,112},{112,96},{1... | collective-permute-start | bytes 110600 | tf_op jit(solution)/shard_map/ppermute | solution.py:190
  1.8 5.4 %collective-permute-start.1 = (bf16[384,96]{1,0:T(8,128)(2,1)S(1)}, bf16[384,96]{1,0:T(8,128)(2,1)S(1)}, u32[]{:S(2)}, u32[]{:S(2)}) collective-permute-start(bf16[384,96]{1,0:T(8,128)(2,1)S(1)} %constant_dynamic-update-slice_fusion.p0), channel_id=1, source_target_pairs={{0,32},{16,48},{32,64},{48,80},{64,96},{80,112},{96,0},{112,16},{1... | collective-permute-start | bytes 221192 | tf_op jit(solution)/shard_map/ppermute | solution.py:191
  3.1 7.3 %collective-permute-start.2 = (bf16[384,96]{1,0:T(8,128)(2,1)S(1)}, bf16[384,96]{1,0:T(8,128)(2,1)S(1)}, u32[]{:S(2)}, u32[]{:S(2)}) collective-permute-start(bf16[384,96]{1,0:T(8,128)(2,1)S(1)} %constant_dynamic-update-slice_fusion.p0), channel_id=1, source_target_pairs={{0,64},{16,80},{32,96},{48,112},{64,0},{80,16},{96,32},{112,48},{1... | collective-permute-start | bytes 221192 | tf_op jit(solution)/shard_map/ppermute | solution.py:191
  5.8 4.7 %collective-permute-start.3 = (bf16[384,96]{1,0:T(8,128)(2,1)S(1)}, bf16[384,96]{1,0:T(8,128)(2,1)S(1)}, u32[]{:S(2)}, u32[]{:S(2)}) collective-permute-start(bf16[384,96]{1,0:T(8,128)(2,1)S(1)} %constant_dynamic-update-slice_fusion.p0), channel_id=1, source_target_pairs={{0,96},{16,112},{32,0},{48,16},{64,32},{80,48},{96,64},{112,80},{1... | collective-permute-start | bytes 221192 | tf_op jit(solution)/shard_map/ppermute | solution.py:191
  10.4 0.7 copy-start
  11.1 0.7 copy-start.2
  13.2 3.8 %collective-permute-start.4 = (bf16[96,640]{1,0:T(8,128)(2,1)S(1)}, bf16[96,640]{1,0:T(8,128)(2,1)S(1)}, u32[]{:S(2)}, u32[]{:S(2)}) collective-permute-start(bf16[96,640]{1,0:T(8,128)(2,1)S(1)} %select.3), channel_id=1, source_target_pairs={{0,1},{1,2},{2,3},{3,0},{4,5},{5,6},{6,7},{7,4},{8,9},{9,10},{10,1... | collective-permute-start | bytes 368648 | tf_op jit(solution)/shard_map/ppermute | solution.py:221
  14.6 5.5 %collective-permute-start.5 = (bf16[96,640]{1,0:T(8,128)(2,1)S(1)}, bf16[96,640]{1,0:T(8,128)(2,1)S(1)}, u32[]{:S(2)}, u32[]{:S(2)}) collective-permute-start(bf16[96,640]{1,0:T(8,128)(2,1)S(1)} %select.3), channel_id=1, source_target_pairs={{0,2},{1,3},{2,0},{3,1},{4,6},{5,7},{6,4},{7,5},{8,10},{9,11},{10,... | collective-permute-start | bytes 368648 | tf_op jit(solution)/shard_map/ppermute | solution.py:221
  14.6 5.5 %collective-permute-start.6 = (bf16[96,640]{1,0:T(8,128)(2,1)S(1)}, bf16[96,640]{1,0:T(8,128)(2,1)S(1)}, u32[]{:S(2)}, u32[]{:S(2)}) collective-permute-start(bf16[96,640]{1,0:T(8,128)(2,1)S(1)} %select.3), channel_id=1, source_target_pairs={{0,3},{1,0},{2,1},{3,2},{4,7},{5,4},{6,5},{7,6},{8,11},{9,8},{10,9... | collective-permute-start | bytes 368648 | tf_op jit(solution)/shard_map/ppermute | solution.py:221
  20.2 9.1 %collective-permute-start.7 = (bf16[384,640]{1,0:T(8,128)(2,1)S(1)}, bf16[384,640]{1,0:T(8,128)(2,1)S(1)}, u32[]{:S(2)}, u32[]{:S(2)}) collective-permute-start(bf16[384,640]{1,0:T(8,128)(2,1)S(1)} %pad_maximum_fusion.q0), channel_id=1, source_target_pairs={{0,4},{1,5},{2,6},{3,7},{4,8},{5,9},{6,10},{7,11},{8,12},{9,13},{1... | collective-permute-start | bytes 1474568 | tf_op jit(solution)/shard_map/ppermute | solution.py:223
  21.7 13.9 %collective-permute-start.8 = (bf16[384,640]{1,0:T(8,128)(2,1)S(1)}, bf16[384,640]{1,0:T(8,128)(2,1)S(1)}, u32[]{:S(2)}, u32[]{:S(2)}) collective-permute-start(bf16[384,640]{1,0:T(8,128)(2,1)S(1)} %pad_maximum_fusion.q0), channel_id=1, source_target_pairs={{0,8},{1,9},{2,10},{3,11},{4,12},{5,13},{6,14},{7,15},{8,0},{9,1},... | collective-permute-start | bytes 1474568 | tf_op jit(solution)/shard_map/ppermute | solution.py:223
  24.2 11.5 %collective-permute-start.9 = (bf16[384,640]{1,0:T(8,128)(2,1)S(1)}, bf16[384,640]{1,0:T(8,128)(2,1)S(1)}, u32[]{:S(2)}, u32[]{:S(2)}) collective-permute-start(bf16[384,640]{1,0:T(8,128)(2,1)S(1)} %pad_maximum_fusion.q0), channel_id=1, source_target_pairs={{0,12},{1,13},{2,14},{3,15},{4,0},{5,1},{6,2},{7,3},{8,4},{9,5},{1... | collective-permute-start | bytes 1474568 | tf_op jit(solution)/shard_map/ppermute | solution.py:223
  35.7 0.7 copy-start.1
  36.3 0.7 copy-start.3
  92.2 6.4 %collective-permute-start.10 = (f32[4,192,96]{2,1,0:T(8,128)S(1)}, f32[4,192,96]{2,1,0:T(8,128)S(1)}, u32[]{:S(2)}, u32[]{:S(2)}) collective-permute-start(f32[4,192,96]{2,1,0:T(8,128)S(1)} %get-tuple-element.8), channel_id=1, source_target_pairs={{0,16},{16,0},{32,48},{48,32},{64,80},{80,64},{96,112},{112,96},{1... | collective-permute-start | bytes 884744 | tf_op jit(solution)/shard_map/ppermute | solution.py:260
  98.6 5.3 %collective-permute-start.11 = (f32[192,96]{1,0:T(8,128)S(1)}, f32[192,96]{1,0:T(8,128)S(1)}, u32[]{:S(2)}, u32[]{:S(2)}) collective-permute-start(f32[192,96]{1,0:T(8,128)S(1)} %get-tuple-element.9), channel_id=1, source_target_pairs={{0,32},{16,48},{32,64},{48,80},{64,96},{80,112},{96,0},{112,16},{1... | collective-permute-start | bytes 221192 | tf_op jit(solution)/shard_map/ppermute | solution.py:263
  99.3 6.8 %collective-permute-start.12 = (f32[192,96]{1,0:T(8,128)S(1)}, f32[192,96]{1,0:T(8,128)S(1)}, u32[]{:S(2)}, u32[]{:S(2)}) collective-permute-start(f32[192,96]{1,0:T(8,128)S(1)} %get-tuple-element.11), channel_id=1, source_target_pairs={{0,64},{16,80},{32,96},{48,112},{64,0},{80,16},{96,32},{112,48},{1... | collective-permute-start | bytes 221192 | tf_op jit(solution)/shard_map/ppermute | solution.py:263
  101.5 4.8 %collective-permute-start.13 = (f32[192,96]{1,0:T(8,128)S(1)}, f32[192,96]{1,0:T(8,128)S(1)}, u32[]{:S(2)}, u32[]{:S(2)}) collective-permute-start(f32[192,96]{1,0:T(8,128)S(1)} %get-tuple-element.10), channel_id=1, source_target_pairs={{0,96},{16,112},{32,0},{48,16},{64,32},{80,48},{96,64},{112,80},{1... | collective-permute-start | bytes 221192 | tf_op jit(solution)/shard_map/ppermute | solution.py:263
  106.3 12.0 %collective-permute-start.14 = (f32[96,96]{1,0:T(8,128)S(1)}, f32[96,96]{1,0:T(8,128)S(1)}, u32[]{:S(2)}, u32[]{:S(2)}) collective-permute-start(f32[96,96]{1,0:T(8,128)S(1)} %get-tuple-element.13), channel_id=1, source_target_pairs={{0,0},{1,1},{2,16},{3,17},{4,32},{5,33},{6,48},{7,49},{8,64},{9,65... | collective-permute-start | bytes 110600 | tf_op jit(solution)/shard_map/ppermute | solution.py:269
  113.6 10.1 %collective-permute-start.15 = (f32[96,96]{1,0:T(8,128)S(1)}, f32[96,96]{1,0:T(8,128)S(1)}, u32[]{:S(2)}, u32[]{:S(2)}) collective-permute-start(f32[96,96]{1,0:T(8,128)S(1)} %get-tuple-element.12), channel_id=1, source_target_pairs={{0,1},{1,0},{2,17},{3,16},{4,33},{5,32},{6,49},{7,48},{8,65},{9,64... | collective-permute-start | bytes 110600 | tf_op jit(solution)/shard_map/ppermute | solution.py:270

commit v3 on v2

--- a/solution.py
+++ b/solution.py
@@ -17,6 +17,10 @@
 ND = NG // 2 + 1
 WIDTH = KN * BS
 KEEP = ND * LANES
+FAR = (ND - 1) * LANES
+HB = BS // 2
+PANEL = 3 * (BS * (ND - 1) + HB)
+TAIL = 3 * BS * (ND - 1)
 MIB = 1 << 20
 
 
@@ -29,6 +33,24 @@
     for k in range(KN):
         index = jnp.where(slot_of[nb[0, k]] == storage, k, index)
     return index
+
+
+def far_half(index):
+    late = (index // (KN // 2)) % 2
+    upper = (index % GB) // (GB // 2)
+    return (upper + late) % 2
+
+
+def pack_far(tile, half):
+    turn = pltpu.roll(tile, LANES // 2, 1)
+    left = lax.broadcasted_iota(jnp.int32, (HB, LANES), 1) < LANES // 2
+    low = jnp.where(half == 0, tile, turn)[:HB]
+    high = jnp.where(half == 0, turn, tile)[HB:]
+    return jnp.where(left, low, high)
+
+
+def unpack_far(packed):
+    return jnp.concatenate([packed, pltpu.roll(packed, LANES // 2, 1)], axis=0)
 
 
 def select_kernel(ny, ncol, rows, nb, slot_of, p0, p1, p2, p3, out, panel, chosen, turned, sem):
@@ -64,7 +86,16 @@
         index = find(slot_of, nb, col * per + j)
         group = jnp.where(index < KN, index // GB, 0)
         start = pl.multiple_of(group * LANES, LANES)
-        out[j * BS : (j + 1) * BS, :] = turned[j * BS : (j + 1) * BS, pl.ds(start, KEEP)]
+        lines = turned[j * BS : (j + 1) * BS, pl.ds(start, KEEP)]
+        for d in range(ND - 1):
+            r = (d * per + j) * BS
+            out[r : r + BS, :] = lines[:, d * LANES : (d + 1) * LANES]
+        far = pack_far(lines[:, FAR:].astype(jnp.float32), far_half(index))
+        out[TAIL + j * HB : TAIL + (j + 1) * HB, :] = far.astype(jnp.bfloat16)
+
+
+def place_of(storage):
+    return (storage // 3) * PANEL, storage % 3
 
 
 def exchange_kernel(side, q0, q1, q2, q3, nb, slot_of, tensor, out, gathered, local, half, acc):
@@ -76,27 +107,40 @@
     def _():
         h = lax.axis_index("row") % 2
         z, x = lax.axis_index("col") // side, lax.axis_index("col") % side
-        cols = gathered.shape[0] // side**2
+        left = lax.broadcasted_iota(jnp.int32, (BS, LANES), 1) < LANES // 2
         for j, part in enumerate((q0, q1, q2, q3)):
             for k in range(side):
                 dz, dx = jnp.where(h == 0, j, k), jnp.where(h == 0, k, j)
                 owner = lax.rem(z - dz + side, side) * side + lax.rem(x - dx + side, side)
-                at = pl.multiple_of(owner * cols, 32)
-                gathered[pl.ds(at, cols), :] = part[k * cols : (k + 1) * cols, :]
+                at = pl.multiple_of(owner * PANEL, 16)
+                gathered[pl.ds(at, PANEL), :] = part[k * PANEL : (k + 1) * PANEL, :]
         for k in range(KN):
-            at = pl.multiple_of(slot_of[nb[0, k]] * BS, BS)
+            base, j = place_of(slot_of[nb[0, k]])
             group = k // GB
-            for d in range(ND):
+            for d in range(ND - 1):
                 to = (group + d) % NG
-                local[k * BS : (k + 1) * BS, to * LANES : (to + 1) * LANES] = gathered[
-                    pl.ds(at, BS), d * LANES : (d + 1) * LANES
-                ]
+                at = pl.multiple_of(base + (d * 3 + j) * BS, 16)
+                local[k * BS : (k + 1) * BS, to * LANES : (to + 1) * LANES] = gathered[pl.ds(at, BS), :]
+            at = pl.multiple_of(base + TAIL + j * HB, 16)
+            tile = unpack_far(gathered[pl.ds(at, HB), :].astype(jnp.float32))
+            if far_half(k):
+                tile = jnp.where(left, 0.0, pltpu.roll(tile, LANES // 2, 1))
+            else:
+                tile = jnp.where(left, tile, 0.0)
+            to = (group + NG // 2) % NG
+            local[k * BS : (k + 1) * BS, to * LANES : (to + 1) * LANES] = tile.astype(jnp.bfloat16)
         for group in range(NG):
+            here = slice(group * LANES, (group + 1) * LANES)
             for d in range(1, NG // 2):
                 to = (group + d) % NG
-                local[to * LANES : (to + 1) * LANES, group * LANES : (group + 1) * LANES] = local[
-                    group * LANES : (group + 1) * LANES, to * LANES : (to + 1) * LANES
-                ].T
+                there = slice(to * LANES, (to + 1) * LANES)
+                local[there, here] = local[here, there].T
+        for group in range(NG // 2):
+            here = slice(group * LANES, (group + 1) * LANES)
+            there = slice((group + NG // 2) * LANES, (group + NG // 2 + 1) * LANES)
+            tile = local[here, there] + local[there, here].T
+            local[here, there] = tile
+            local[there, here] = tile.T
         acc[...] = jnp.zeros_like(acc)
 
     for i in range(tiles):
@@ -120,12 +164,16 @@
         scale = 1.0 + lax.axis_index("col").astype(jnp.float32) / ncol
         out[...] = jnp.zeros_like(out)
         for k in range(KN):
-            at = pl.multiple_of(slot_of[nb[0, k]] * BS, BS)
+            base, j = place_of(slot_of[nb[0, k]])
             group = k // GB
             i, odd = group // 2, group % 2
             r = (k % (2 * GB)) * BS
-            piece = acc[i, r : r + BS, odd * LANES : odd * LANES + KEEP]
-            out[pl.ds(at, BS), :] = (piece * scale).astype(jnp.bfloat16)
+            piece = acc[i, r : r + BS, odd * LANES : odd * LANES + KEEP] * scale
+            for d in range(ND - 1):
+                at = pl.multiple_of(base + (d * 3 + j) * BS, 16)
+                out[pl.ds(at, BS), :] = piece[:, d * LANES : (d + 1) * LANES].astype(jnp.bfloat16)
+            at = pl.multiple_of(base + TAIL + j * HB, 16)
+            out[pl.ds(at, HB), :] = pack_far(piece[:, FAR:], far_half(k)).astype(jnp.bfloat16)
 
 
 def place_kernel(ny, ncol, rows, nb, slot_of, parts, mine, other, total, turned, placed):
@@ -136,10 +184,12 @@
     sums = parts[0].astype(jnp.float32)
     for i in range(1, ncol):
         sums += parts[i].astype(jnp.float32) * (1.0 / (1.0 + i / ncol))
-    total[:96, :] = sums
-    for d in range(ND):
-        tile = total[:, d * LANES : (d + 1) * LANES].T
-        turned[d * LANES : (d + 1) * LANES, :] = tile * 0.5 if d in (0, NG // 2) else tile
+    total[...] = sums
+    for d in range(ND - 1):
+        tile = total[d * per * BS : (d + 1) * per * BS, :].T
+        turned[d * LANES : (d + 1) * LANES, :] = tile * 0.5 if d == 0 else tile
+    far = [unpack_far(total[TAIL + j * HB : TAIL + (j + 1) * HB, :]) for j in range(per)]
+    turned[FAR:, :] = jnp.concatenate(far, axis=0).T
     placed[...] = jnp.zeros_like(placed)
     for j in range(per):
         index = find(slot_of, nb, col * per + j)
@@ -149,8 +199,9 @@
             group = index // GB
             for d in range(ND):
                 to = lax.rem(group + d, NG)
-                for b in range(GB):
-                    at = pl.multiple_of(slot_of[nb[0, to * GB + b]] * BS, BS)
+                for b in range(GB if d < ND - 1 else GB // 2):
+                    first = 0 if d < ND - 1 else far_half(index) * (GB // 2)
+                    at = pl.multiple_of(slot_of[nb[0, to * GB + first + b]] * BS, BS)
                     r = d * LANES + b * BS
                     placed[pl.ds(at, BS), j * BS : (j + 1) * BS] = turned[
                         r : r + BS, j * BS : (j + 1) * BS
@@ -191,7 +242,7 @@
     others = [lax.ppermute(pair, "row", along(k)) for k in range(1, ny)]
     block = pl.pallas_call(
         functools.partial(select_kernel, ny, ncol, rows),
-        out_shape=jax.ShapeDtypeStruct((cols, KEEP), jnp.bfloat16),
+        out_shape=jax.ShapeDtypeStruct((PANEL, LANES), jnp.bfloat16),
         in_specs=[SMEM, SMEM] + [ANY] * 4,
         out_specs=VMEM,
         scratch_shapes=[
@@ -225,7 +276,7 @@
     nfun = tensor.shape[0]
     sent = pl.pallas_call(
         functools.partial(exchange_kernel, side),
-        out_shape=jax.ShapeDtypeStruct((total, KEEP), jnp.bfloat16),
+        out_shape=jax.ShapeDtypeStruct((ncol * PANEL, LANES), jnp.bfloat16),
         grid=(nfun,),
         in_specs=[pl.BlockSpec(line.shape, lambda p: (0, 0))] * side
         + [
@@ -233,9 +284,9 @@
             SMEM,
             pl.BlockSpec((1, WIDTH, WIDTH), lambda p: (p, 0, 0)),
         ],
-        out_specs=pl.BlockSpec((total, KEEP), lambda p: (0, 0)),
+        out_specs=pl.BlockSpec((ncol * PANEL, LANES), lambda p: (0, 0)),
         scratch_shapes=[
-            pltpu.VMEM((total, KEEP), jnp.bfloat16),
+            pltpu.VMEM((ncol * PANEL, LANES), jnp.bfloat16),
             pltpu.VMEM((WIDTH, WIDTH), jnp.bfloat16),
             pltpu.VMEM((WIDTH, WIDTH), jnp.bfloat16),
             pltpu.VMEM((4, 2 * LANES, 6 * LANES), jnp.float32),
@@ -243,15 +294,15 @@
         compiler_params=params(48),
         name="exchange",
     )(*plane, neighbors, atom_slot, tensor)
-    parts = lax.all_to_all(sent.reshape(ncol, cols, KEEP), "col", 0, 0, tiled=True)
+    parts = lax.all_to_all(sent.reshape(ncol, PANEL, LANES), "col", 0, 0, tiled=True)
     mine, other = pl.pallas_call(
         functools.partial(place_kernel, ny, ncol, rows),
         out_shape=[jax.ShapeDtypeStruct((ny, rows, cols), jnp.float32)] * 2,
         in_specs=[SMEM, SMEM, VMEM],
         out_specs=[VMEM, VMEM],
         scratch_shapes=[
-            pltpu.VMEM((LANES, KEEP), jnp.float32),
-            pltpu.VMEM((KEEP, LANES), jnp.float32),
+            pltpu.VMEM((PANEL, LANES), jnp.float32),
+            pltpu.VMEM((KEEP, cols), jnp.float32),
             pltpu.VMEM((total, cols), jnp.float32),
         ],
         compiler_params=params(12),

time: 125 us -> 122 us (0.976)
  blocking collectives: 27.3 us -> 24.8 us
    all_to_all x1, blocking collectives: 27.3 us -> 24.8 us  [shards(): lax.all_to_all(sent.reshape(ncol, PANEL, LANES), 'col', 0, 0, tiled=True)]
where the time goes in v3:
time: 122 us
  starting transfers between devices  32.6 us (27%)
  Pallas kernels  31 us (25%)
  waiting for transfers between devices  30.4 us (25%)
  blocking collectives  24.8 us (20%)
  local copies, waits for them, and re-layouts  3.45 us (3%)
    pallas_call x1, Pallas kernels, shards(): pl.pallas_call(functools.partial(exchange_kernel, side), out_shape=jax.Sh...  27.5 us
    all_to_all x1, blocking collectives, shards(): lax.all_to_all(sent.reshape(ncol, PANEL, LANES), 'col', 0, 0, tiled=True)  24.8 us
    ppermute x3, waiting for transfers between devices, shards(): lax.ppermute(line, both, stage(k, False))  9.57 us
    ppermute x1, starting transfers between devices, shards(): first = lax.ppermute(jnp.where(b == 0, upper, lower), ('row', 'col'), same)  7.76 us
    ppermute x1, waiting for transfers between devices, shards(): second = lax.ppermute(jnp.where(b == 0, lower, upper), ('row', 'col'), swap)  5.98 us
    ppermute x1, starting transfers between devices, shards(): chip = mine + lax.ppermute(other, 'row', core)  5.34 us
    ppermute x3, starting transfers between devices, shards(): others = [lax.ppermute(pair, 'row', along(k)) for k in range(1, ny)]  5.05 us
    ppermute x3, starting transfers between devices, shards(): lax.ppermute(line, both, stage(k, False))  4.75 us
  transfers between devices with their start and end apart: 16, of which 13 were waited for; matrix products, arithmetic and copies ran while one was open for 1% of the time, Pallas kernels for 0%

profile of v3, /device:TPU:65, one launch (start us, length us, event | category | flops | bytes accessed | tf_op | source)
XLA Modules:
  0.0 122.3 jit_solution(219321789116758871)
XLA Ops:
  1.8 1.4 %collective-permute-start.1 = (bf16[384,96]{1,0:T(8,128)(2,1)S(1)}, bf16[384,96]{1,0:T(8,128)(2,1)S(1)}, u32[]{:S(2)}, u32[]{:S(2)}) collective-permute-start(bf16[384,96]{1,0:T(8,128)(2,1)S(1)} %constant_dynamic-update-slice_fusion.p0), channel_id=1, source_target_pairs={{0,32},{16,48},{32,64},{48,80},{64,96},{80,112},{96,0},{112,16},{1... | collective-permute-start | bytes 221192 | tf_op jit(solution)/shard_map/ppermute | solution.py:242
  3.1 2.6 %collective-permute-start.2 = (bf16[384,96]{1,0:T(8,128)(2,1)S(1)}, bf16[384,96]{1,0:T(8,128)(2,1)S(1)}, u32[]{:S(2)}, u32[]{:S(2)}) collective-permute-start(bf16[384,96]{1,0:T(8,128)(2,1)S(1)} %constant_dynamic-update-slice_fusion.p0), channel_id=1, source_target_pairs={{0,64},{16,80},{32,96},{48,112},{64,0},{80,16},{96,32},{112,48},{1... | collective-permute-start | bytes 221192 | tf_op jit(solution)/shard_map/ppermute | solution.py:242
  7.2 3.2 %collective-permute-done.2.p2 = bf16[384,96]{1,0:T(8,128)(2,1)S(1)} collective-permute-done((bf16[384,96]{1,0:T(8,128)(2,1)S(1)}, bf16[384,96]{1,0:T(8,128)(2,1)S(1)}, u32[]{:S(2)}, u32[]{:S(2)}) %collective-permute-start.2) | collective-permute-done | bytes 73760 | tf_op jit(solution)/shard_map/ppermute | solution.py:242
  11.7 1.5 %select.3 = bf16[432,128]{1,0:T(8,128)(2,1)S(1)} custom-call(s32[1,32]{1,0:T(1,128)S(1)} %copy-done, s32[48]{0:T(128)S(1)} %copy-done.2, bf16[384,96]{1,0:T(8,128)(2,1)S(1)} %constant_dynamic-update-slice_fusion.p0, bf16[384,96]{1,0:T(8,128)(2,1)S(1)} %collective-permute-done.1.p1, bf16[384,96]{1,0:T(8,128)(2,1)S(1)} %collective-permute-done.2.p2, ...), custom_call_target="tpu_custom_call" | custom-call | tf_op jit(solution)/shard_map/select/pallas_call | solution.py:243
  13.2 1.4 %collective-permute-start.4 = (bf16[432,128]{1,0:T(8,128)(2,1)S(1)}, bf16[432,128]{1,0:T(8,128)(2,1)S(1)}, u32[]{:S(2)}, u32[]{:S(2)}) collective-permute-start(bf16[432,128]{1,0:T(8,128)(2,1)S(1)} %select.3), channel_id=1, source_target_pairs={{0,1},{1,2},{2,3},{3,0},{4,5},{5,6},{6,7},{7,4},{8,9},{9,10},{10,1... | collective-permute-start | bytes 331784 | tf_op jit(solution)/shard_map/ppermute | solution.py:272
  14.6 1.3 %collective-permute-start.6 = (bf16[432,128]{1,0:T(8,128)(2,1)S(1)}, bf16[432,128]{1,0:T(8,128)(2,1)S(1)}, u32[]{:S(2)}, u32[]{:S(2)}) collective-permute-start(bf16[432,128]{1,0:T(8,128)(2,1)S(1)} %select.3), channel_id=1, source_target_pairs={{0,3},{1,0},{2,1},{3,2},{4,7},{5,4},{6,5},{7,6},{8,11},{9,8},{10,9... | collective-permute-start | bytes 331784 | tf_op jit(solution)/shard_map/ppermute | solution.py:272
  16.9 3.1 %collective-permute-done.5 = bf16[432,128]{1,0:T(8,128)(2,1)S(1)} collective-permute-done((bf16[432,128]{1,0:T(8,128)(2,1)S(1)}, bf16[432,128]{1,0:T(8,128)(2,1)S(1)}, u32[]{:S(2)}, u32[]{:S(2)}) %collective-permute-start.5) | collective-permute-done | bytes 110624 | tf_op jit(solution)/shard_map/ppermute | solution.py:272
  20.1 1.2 collective-permute-start.7
  21.2 2.7 %collective-permute-start.8 = (bf16[1728,128]{1,0:T(8,128)(2,1)S(1)}, bf16[1728,128]{1,0:T(8,128)(2,1)S(1)}, u32[]{:S(2)}, u32[]{:S(2)}) collective-permute-start(bf16[1728,128]{1,0:T(8,128)(2,1)S(1)} %pad_maximum_fusion.q0), channel_id=1, source_target_pairs={{0,8},{1,9},{2,10},{3,11},{4,12},{5,13},{6,14},{7,15},{8,0},{9,1},... | collective-permute-start | bytes 1327112 | tf_op jit(solution)/shard_map/ppermute | solution.py:274
  24.8 3.7 %collective-permute-done.7.q1 = bf16[1728,128]{1,0:T(8,128)(2,1)S(1)} collective-permute-done((bf16[1728,128]{1,0:T(8,128)(2,1)S(1)}, bf16[1728,128]{1,0:T(8,128)(2,1)S(1)}, u32[]{:S(2)}, u32[]{:S(2)}) %collective-permute-start.7) | collective-permute-done | bytes 442400 | tf_op jit(solution)/shard_map/ppermute | solution.py:274
  28.5 5.9 %collective-permute-done.8.q2 = bf16[1728,128]{1,0:T(8,128)(2,1)S(1)} collective-permute-done((bf16[1728,128]{1,0:T(8,128)(2,1)S(1)}, bf16[1728,128]{1,0:T(8,128)(2,1)S(1)}, u32[]{:S(2)}, u32[]{:S(2)}) %collective-permute-start.8) | collective-permute-done | bytes 442400 | tf_op jit(solution)/shard_map/ppermute | solution.py:274
  35.7 27.5 %exchange.1 = bf16[6912,128]{1,0:T(8,128)(2,1)S(1)} custom-call(bf16[1728,128]{1,0:T(8,128)(2,1)S(1)} %pad_maximum_fusion.q0, bf16[1728,128]{1,0:T(8,128)(2,1)S(1)} %collective-permute-done.7.q1, bf16[1728,128]{1,0:T(8,128)(2,1)S(1)} %collective-permute-done.8.q2, bf16[1728,128]{1,0:T(8,128)(2,1)S(1)} %collective-permute-done.9.q3, s32[1,32]{1,0:T(1,128)S(1)} %copy-done.1, ...), custom_call_target="tpu_custom_call" | custom-call | tf_op jit(solution)/shard_map/exchange/pallas_call | solution.py:277
  63.2 24.8 %all_to_all.5.parts = bf16[16,432,128]{2,1,0:T(8,128)(2,1)S(1)} all-to-all(bf16[16,432,128]{2,1,0:T(8,128)(2,1)S(1)} %bitcast.16), channel_id=1, replica_groups=mesh['row'=8,'col'=16] {'col'}, dimensions={0} | all-to-all | bytes 3538944 | tf_op jit(solution)/shard_map/all_to_all | solution.py:297
  88.0 1.3 %place.1 = (f32[4,192,96]{2,1,0:T(8,128)S(1)}, f32[4,192,96]{2,1,0:T(8,128)S(1)}) custom-call(s32[1,32]{1,0:T(1,128)S(1)} %copy-done.1, s32[48]{0:T(128)S(1)} %copy-done.3, bf16[16,432,128]{2,1,0:T(8,128)(2,1)S(1)} %all_to_all.5.parts), custom_call_target="tpu_custom_call" | custom-call | tf_op jit(solution)/shard_map/place/pallas_call | solution.py:298
  89.3 5.3 %collective-permute-start.10 = (f32[4,192,96]{2,1,0:T(8,128)S(1)}, f32[4,192,96]{2,1,0:T(8,128)S(1)}, u32[]{:S(2)}, u32[]{:S(2)}) collective-permute-start(f32[4,192,96]{2,1,0:T(8,128)S(1)} %get-tuple-element.8), channel_id=1, source_target_pairs={{0,16},{16,0},{32,48},{48,32},{64,80},{80,64},{96,112},{112,96},{1... | collective-permute-start | bytes 884744 | tf_op jit(solution)/shard_map/ppermute | solution.py:311
  94.6 1.3 %collective-permute-done.10 = f32[4,192,96]{2,1,0:T(8,128)S(1)} collective-permute-done((f32[4,192,96]{2,1,0:T(8,128)S(1)}, f32[4,192,96]{2,1,0:T(8,128)S(1)}, u32[]{:S(2)}, u32[]{:S(2)}) %collective-permute-start.10) | collective-permute-done | bytes 294944 | tf_op jit(solution)/shard_map/ppermute | solution.py:311
  96.9 2.1 %collective-permute-start.12 = (f32[192,96]{1,0:T(8,128)S(1)}, f32[192,96]{1,0:T(8,128)S(1)}, u32[]{:S(2)}, u32[]{:S(2)}) collective-permute-start(f32[192,96]{1,0:T(8,128)S(1)} %get-tuple-element.11), channel_id=1, source_target_pairs={{0,64},{16,80},{32,96},{48,112},{64,0},{80,16},{96,32},{112,48},{1... | collective-permute-start | bytes 221192 | tf_op jit(solution)/shard_map/ppermute | solution.py:314
  99.0 1.3 %collective-permute-start.13 = (f32[192,96]{1,0:T(8,128)S(1)}, f32[192,96]{1,0:T(8,128)S(1)}, u32[]{:S(2)}, u32[]{:S(2)}) collective-permute-start(f32[192,96]{1,0:T(8,128)S(1)} %get-tuple-element.10), channel_id=1, source_target_pairs={{0,96},{16,112},{32,0},{48,16},{64,32},{80,48},{96,64},{112,80},{1... | collective-permute-start | bytes 221192 | tf_op jit(solution)/shard_map/ppermute | solution.py:314
  100.3 1.1 collective-permute-done.11
  101.3 2.3 %collective-permute-done.12 = f32[192,96]{1,0:T(8,128)S(1)} collective-permute-done((f32[192,96]{1,0:T(8,128)S(1)}, f32[192,96]{1,0:T(8,128)S(1)}, u32[]{:S(2)}, u32[]{:S(2)}) %collective-permute-start.12) | collective-permute-done | bytes 73760 | tf_op jit(solution)/shard_map/ppermute | solution.py:314
  103.7 7.8 %collective-permute-start.14 = (f32[96,96]{1,0:T(8,128)S(1)}, f32[96,96]{1,0:T(8,128)S(1)}, u32[]{:S(2)}, u32[]{:S(2)}) collective-permute-start(f32[96,96]{1,0:T(8,128)S(1)} %get-tuple-element.13), channel_id=1, source_target_pairs={{0,0},{1,1},{2,16},{3,17},{4,32},{5,33},{6,48},{7,49},{8,64},{9,65... | collective-permute-start | bytes 110600 | tf_op jit(solution)/shard_map/ppermute | solution.py:320
  111.5 2.1 %collective-permute-start.15 = (f32[96,96]{1,0:T(8,128)S(1)}, f32[96,96]{1,0:T(8,128)S(1)}, u32[]{:S(2)}, u32[]{:S(2)}) collective-permute-start(f32[96,96]{1,0:T(8,128)S(1)} %get-tuple-element.12), channel_id=1, source_target_pairs={{0,1},{1,0},{2,17},{3,16},{4,33},{5,32},{6,49},{7,48},{8,65},{9,64... | collective-permute-start | bytes 110600 | tf_op jit(solution)/shard_map/ppermute | solution.py:321
  113.6 2.0 %collective-permute-done.14.first = f32[96,96]{1,0:T(8,128)S(1)} collective-permute-done((f32[96,96]{1,0:T(8,128)S(1)}, f32[96,96]{1,0:T(8,128)S(1)}, u32[]{:S(2)}, u32[]{:S(2)}) %collective-permute-start.14) | collective-permute-done | bytes 36896 | tf_op jit(solution)/shard_map/ppermute | solution.py:320
  115.6 6.0 %collective-permute-done.15.second = f32[96,96]{1,0:T(8,128)S(1)} collective-permute-done((f32[96,96]{1,0:T(8,128)S(1)}, f32[96,96]{1,0:T(8,128)S(1)}, u32[]{:S(2)}, u32[]{:S(2)}) %collective-permute-start.15) | collective-permute-done | bytes 36896 | tf_op jit(solution)/shard_map/ppermute | solution.py:321
  (28 shorter events, 9.5 us)
Async XLA Ops:
  0.0 1.8 %collective-permute-start = (bf16[192,96]{1,0:T(8,128)(2,1)}, bf16[192,96]{1,0:T(8,128)(2,1)S(1)}, u32[]{:S(2)}, u32[]{:S(2)}) collective-permute-start(bf16[192,96]{1,0:T(8,128)(2,1)} %param.5), channel_id=1, source_target_pairs={{0,16},{16,0},{32,48},{48,32},{64,80},{80,64},{96,112},{112,96},{1... | collective-permute-start | bytes 110600 | tf_op jit(solution)/shard_map/ppermute | solution.py:241
  1.8 5.4 %collective-permute-start.1 = (bf16[384,96]{1,0:T(8,128)(2,1)S(1)}, bf16[384,96]{1,0:T(8,128)(2,1)S(1)}, u32[]{:S(2)}, u32[]{:S(2)}) collective-permute-start(bf16[384,96]{1,0:T(8,128)(2,1)S(1)} %constant_dynamic-update-slice_fusion.p0), channel_id=1, source_target_pairs={{0,32},{16,48},{32,64},{48,80},{64,96},{80,112},{96,0},{112,16},{1... | collective-permute-start | bytes 221192 | tf_op jit(solution)/shard_map/ppermute | solution.py:242
  3.1 7.3 %collective-permute-start.2 = (bf16[384,96]{1,0:T(8,128)(2,1)S(1)}, bf16[384,96]{1,0:T(8,128)(2,1)S(1)}, u32[]{:S(2)}, u32[]{:S(2)}) collective-permute-start(bf16[384,96]{1,0:T(8,128)(2,1)S(1)} %constant_dynamic-update-slice_fusion.p0), channel_id=1, source_target_pairs={{0,64},{16,80},{32,96},{48,112},{64,0},{80,16},{96,32},{112,48},{1... | collective-permute-start | bytes 221192 | tf_op jit(solution)/shard_map/ppermute | solution.py:242
  5.8 4.7 %collective-permute-start.3 = (bf16[384,96]{1,0:T(8,128)(2,1)S(1)}, bf16[384,96]{1,0:T(8,128)(2,1)S(1)}, u32[]{:S(2)}, u32[]{:S(2)}) collective-permute-start(bf16[384,96]{1,0:T(8,128)(2,1)S(1)} %constant_dynamic-update-slice_fusion.p0), channel_id=1, source_target_pairs={{0,96},{16,112},{32,0},{48,16},{64,32},{80,48},{96,64},{112,80},{1... | collective-permute-start | bytes 221192 | tf_op jit(solution)/shard_map/ppermute | solution.py:242
  10.4 0.7 copy-start
  11.1 0.7 copy-start.2
  13.2 3.7 %collective-permute-start.4 = (bf16[432,128]{1,0:T(8,128)(2,1)S(1)}, bf16[432,128]{1,0:T(8,128)(2,1)S(1)}, u32[]{:S(2)}, u32[]{:S(2)}) collective-permute-start(bf16[432,128]{1,0:T(8,128)(2,1)S(1)} %select.3), channel_id=1, source_target_pairs={{0,1},{1,2},{2,3},{3,0},{4,5},{5,6},{6,7},{7,4},{8,9},{9,10},{10,1... | collective-permute-start | bytes 331784 | tf_op jit(solution)/shard_map/ppermute | solution.py:272
  14.6 5.4 %collective-permute-start.5 = (bf16[432,128]{1,0:T(8,128)(2,1)S(1)}, bf16[432,128]{1,0:T(8,128)(2,1)S(1)}, u32[]{:S(2)}, u32[]{:S(2)}) collective-permute-start(bf16[432,128]{1,0:T(8,128)(2,1)S(1)} %select.3), channel_id=1, source_target_pairs={{0,2},{1,3},{2,0},{3,1},{4,6},{5,7},{6,4},{7,5},{8,10},{9,11},{10,... | collective-permute-start | bytes 331784 | tf_op jit(solution)/shard_map/ppermute | solution.py:272
  14.6 5.4 %collective-permute-start.6 = (bf16[432,128]{1,0:T(8,128)(2,1)S(1)}, bf16[432,128]{1,0:T(8,128)(2,1)S(1)}, u32[]{:S(2)}, u32[]{:S(2)}) collective-permute-start(bf16[432,128]{1,0:T(8,128)(2,1)S(1)} %select.3), channel_id=1, source_target_pairs={{0,3},{1,0},{2,1},{3,2},{4,7},{5,4},{6,5},{7,6},{8,11},{9,8},{10,9... | collective-permute-start | bytes 331784 | tf_op jit(solution)/shard_map/ppermute | solution.py:272
  20.1 8.4 %collective-permute-start.7 = (bf16[1728,128]{1,0:T(8,128)(2,1)S(1)}, bf16[1728,128]{1,0:T(8,128)(2,1)S(1)}, u32[]{:S(2)}, u32[]{:S(2)}) collective-permute-start(bf16[1728,128]{1,0:T(8,128)(2,1)S(1)} %pad_maximum_fusion.q0), channel_id=1, source_target_pairs={{0,4},{1,5},{2,6},{3,7},{4,8},{5,9},{6,10},{7,11},{8,12},{9,13},{1... | collective-permute-start | bytes 1327112 | tf_op jit(solution)/shard_map/ppermute | solution.py:274
  21.2 13.2 %collective-permute-start.8 = (bf16[1728,128]{1,0:T(8,128)(2,1)S(1)}, bf16[1728,128]{1,0:T(8,128)(2,1)S(1)}, u32[]{:S(2)}, u32[]{:S(2)}) collective-permute-start(bf16[1728,128]{1,0:T(8,128)(2,1)S(1)} %pad_maximum_fusion.q0), channel_id=1, source_target_pairs={{0,8},{1,9},{2,10},{3,11},{4,12},{5,13},{6,14},{7,15},{8,0},{9,1},... | collective-permute-start | bytes 1327112 | tf_op jit(solution)/shard_map/ppermute | solution.py:274
  24.0 10.4 %collective-permute-start.9 = (bf16[1728,128]{1,0:T(8,128)(2,1)S(1)}, bf16[1728,128]{1,0:T(8,128)(2,1)S(1)}, u32[]{:S(2)}, u32[]{:S(2)}) collective-permute-start(bf16[1728,128]{1,0:T(8,128)(2,1)S(1)} %pad_maximum_fusion.q0), channel_id=1, source_target_pairs={{0,12},{1,13},{2,14},{3,15},{4,0},{5,1},{6,2},{7,3},{8,4},{9,5},{1... | collective-permute-start | bytes 1327112 | tf_op jit(solution)/shard_map/ppermute | solution.py:274
  34.4 0.7 copy-start.1
  35.1 0.7 copy-start.3
  89.3 6.7 %collective-permute-start.10 = (f32[4,192,96]{2,1,0:T(8,128)S(1)}, f32[4,192,96]{2,1,0:T(8,128)S(1)}, u32[]{:S(2)}, u32[]{:S(2)}) collective-permute-start(f32[4,192,96]{2,1,0:T(8,128)S(1)} %get-tuple-element.8), channel_id=1, source_target_pairs={{0,16},{16,0},{32,48},{48,32},{64,80},{80,64},{96,112},{112,96},{1... | collective-permute-start | bytes 884744 | tf_op jit(solution)/shard_map/ppermute | solution.py:311
  96.0 5.3 %collective-permute-start.11 = (f32[192,96]{1,0:T(8,128)S(1)}, f32[192,96]{1,0:T(8,128)S(1)}, u32[]{:S(2)}, u32[]{:S(2)}) collective-permute-start(f32[192,96]{1,0:T(8,128)S(1)} %get-tuple-element.9), channel_id=1, source_target_pairs={{0,32},{16,48},{32,64},{48,80},{64,96},{80,112},{96,0},{112,16},{1... | collective-permute-start | bytes 221192 | tf_op jit(solution)/shard_map/ppermute | solution.py:314
  96.9 6.7 %collective-permute-start.12 = (f32[192,96]{1,0:T(8,128)S(1)}, f32[192,96]{1,0:T(8,128)S(1)}, u32[]{:S(2)}, u32[]{:S(2)}) collective-permute-start(f32[192,96]{1,0:T(8,128)S(1)} %get-tuple-element.11), channel_id=1, source_target_pairs={{0,64},{16,80},{32,96},{48,112},{64,0},{80,16},{96,32},{112,48},{1... | collective-permute-start | bytes 221192 | tf_op jit(solution)/shard_map/ppermute | solution.py:314
  99.0 4.7 %collective-permute-start.13 = (f32[192,96]{1,0:T(8,128)S(1)}, f32[192,96]{1,0:T(8,128)S(1)}, u32[]{:S(2)}, u32[]{:S(2)}) collective-permute-start(f32[192,96]{1,0:T(8,128)S(1)} %get-tuple-element.10), channel_id=1, source_target_pairs={{0,96},{16,112},{32,0},{48,16},{64,32},{80,48},{96,64},{112,80},{1... | collective-permute-start | bytes 221192 | tf_op jit(solution)/shard_map/ppermute | solution.py:314
  103.7 11.9 %collective-permute-start.14 = (f32[96,96]{1,0:T(8,128)S(1)}, f32[96,96]{1,0:T(8,128)S(1)}, u32[]{:S(2)}, u32[]{:S(2)}) collective-permute-start(f32[96,96]{1,0:T(8,128)S(1)} %get-tuple-element.13), channel_id=1, source_target_pairs={{0,0},{1,1},{2,16},{3,17},{4,32},{5,33},{6,48},{7,49},{8,64},{9,65... | collective-permute-start | bytes 110600 | tf_op jit(solution)/shard_map/ppermute | solution.py:320
  111.5 10.1 %collective-permute-start.15 = (f32[96,96]{1,0:T(8,128)S(1)}, f32[96,96]{1,0:T(8,128)S(1)}, u32[]{:S(2)}, u32[]{:S(2)}) collective-permute-start(f32[96,96]{1,0:T(8,128)S(1)} %get-tuple-element.12), channel_id=1, source_target_pairs={{0,1},{1,0},{2,17},{3,16},{4,33},{5,32},{6,49},{7,48},{8,65},{9,64... | collective-permute-start | bytes 110600 | tf_op jit(solution)/shard_map/ppermute | solution.py:321

commit v4 on v3

--- a/solution.py
+++ b/solution.py
@@ -28,10 +28,10 @@
     return pltpu.CompilerParams(vmem_limit_bytes=mib * MIB)
 
 
-def find(slot_of, nb, storage):
+def find(table, storage):
     index = jnp.int32(KN)
     for k in range(KN):
-        index = jnp.where(slot_of[nb[0, k]] == storage, k, index)
+        index = jnp.where(table[KN + table[k]] == storage, k, index)
     return index
 
 
@@ -53,7 +53,7 @@
     return jnp.concatenate([packed, pltpu.roll(packed, LANES // 2, 1)], axis=0)
 
 
-def select_kernel(ny, ncol, rows, nb, slot_of, p0, p1, p2, p3, out, panel, chosen, turned, sem):
+def select_kernel(ny, ncol, rows, table, p0, p1, p2, p3, out, panel, chosen, turned, sem):
     row = lax.axis_index("row")
     col = lax.axis_index("col")
     y, h = row // 2, row % 2
@@ -74,7 +74,7 @@
     for copy in copies:
         copy.wait()
     for k in range(KN):
-        at = pl.multiple_of(slot_of[nb[0, k]] * BS, BS)
+        at = pl.multiple_of(table[KN + table[k]] * BS, BS)
         chosen[k * BS : (k + 1) * BS, :96] = panel[pl.ds(at, BS), :]
     for i in range(NG):
         tile = chosen[i * LANES : (i + 1) * LANES, :].T
@@ -83,7 +83,7 @@
             turned[:, (NG + i) * LANES : (NG + i + 1) * LANES] = tile
     per = NA // ncol
     for j in range(per):
-        index = find(slot_of, nb, col * per + j)
+        index = find(table, col * per + j)
         group = jnp.where(index < KN, index // GB, 0)
         start = pl.multiple_of(group * LANES, LANES)
         lines = turned[j * BS : (j + 1) * BS, pl.ds(start, KEEP)]
@@ -98,7 +98,7 @@
     return (storage // 3) * PANEL, storage % 3
 
 
-def exchange_kernel(side, q0, q1, q2, q3, nb, slot_of, tensor, out, gathered, local, half, acc):
+def exchange_kernel(side, q0, q1, q2, q3, table, tensor, out, gathered, local, half, acc):
     step = pl.program_id(0)
     big = 2 * LANES
     tiles = WIDTH // big
@@ -115,7 +115,7 @@
                 at = pl.multiple_of(owner * PANEL, 16)
                 gathered[pl.ds(at, PANEL), :] = part[k * PANEL : (k + 1) * PANEL, :]
         for k in range(KN):
-            base, j = place_of(slot_of[nb[0, k]])
+            base, j = place_of(table[KN + table[k]])
             group = k // GB
             for d in range(ND - 1):
                 to = (group + d) % NG
@@ -149,13 +149,13 @@
         ).astype(jnp.bfloat16)
     for i in range(tiles):
         left = tensor[0, i * big : (i + 1) * big, :]
-        first = min(tiles - 1, tiles - i)
+        first, second = ((tiles - 1, 0), (tiles - 1, 0), (2, 0), (1, 1))[i]
         acc[i, :, : first * big] += jnp.dot(
             left, half[:, i * big : (i + first) * big], preferred_element_type=jnp.float32
         )
-        if first < tiles - 1:
-            acc[i, :, first * big :] += jnp.dot(
-                left, half[:, : (tiles - 1 - first) * big], preferred_element_type=jnp.float32
+        if second:
+            acc[i, :, first * big : (first + second) * big] += jnp.dot(
+                left, half[:, : second * big], preferred_element_type=jnp.float32
             )
 
     @pl.when(step == pl.num_programs(0) - 1)
@@ -163,8 +163,10 @@
         ncol = lax.axis_size("col")
         scale = 1.0 + lax.axis_index("col").astype(jnp.float32) / ncol
         out[...] = jnp.zeros_like(out)
+        for i in range(tiles // 2):
+            acc[i + tiles // 2, :, 2 * big :] = acc[i, :, 2 * big :].T
         for k in range(KN):
-            base, j = place_of(slot_of[nb[0, k]])
+            base, j = place_of(table[KN + table[k]])
             group = k // GB
             i, odd = group // 2, group % 2
             r = (k % (2 * GB)) * BS
@@ -176,7 +178,7 @@
             out[pl.ds(at, HB), :] = pack_far(piece[:, FAR:], far_half(k)).astype(jnp.bfloat16)
 
 
-def place_kernel(ny, ncol, rows, nb, slot_of, parts, mine, other, total, turned, placed):
+def place_kernel(ny, ncol, rows, table, parts, mine, other, total, turned, placed):
     row = lax.axis_index("row")
     col = lax.axis_index("col")
     y, h = row // 2, row % 2
@@ -192,7 +194,7 @@
     turned[FAR:, :] = jnp.concatenate(far, axis=0).T
     placed[...] = jnp.zeros_like(placed)
     for j in range(per):
-        index = find(slot_of, nb, col * per + j)
+        index = find(table, col * per + j)
 
         @pl.when(index < KN)
         def _():
@@ -201,7 +203,7 @@
                 to = lax.rem(group + d, NG)
                 for b in range(GB if d < ND - 1 else GB // 2):
                     first = 0 if d < ND - 1 else far_half(index) * (GB // 2)
-                    at = pl.multiple_of(slot_of[nb[0, to * GB + first + b]] * BS, BS)
+                    at = pl.multiple_of(table[KN + table[to * GB + first + b]] * BS, BS)
                     r = d * LANES + b * BS
                     placed[pl.ds(at, BS), j * BS : (j + 1) * BS] = turned[
                         r : r + BS, j * BS : (j + 1) * BS
@@ -238,12 +240,13 @@
     def along(k):
         return [(i, (i + 2 * k) % nrow) for i in range(nrow)]
 
+    table = jnp.concatenate([neighbors[0], atom_slot])
     pair = jnp.concatenate([density, lax.ppermute(density, "row", core)], axis=0)
     others = [lax.ppermute(pair, "row", along(k)) for k in range(1, ny)]
     block = pl.pallas_call(
         functools.partial(select_kernel, ny, ncol, rows),
         out_shape=jax.ShapeDtypeStruct((PANEL, LANES), jnp.bfloat16),
-        in_specs=[SMEM, SMEM] + [ANY] * 4,
+        in_specs=[SMEM] + [ANY] * 4,
         out_specs=VMEM,
         scratch_shapes=[
             pltpu.VMEM((total, cols), jnp.bfloat16),
@@ -253,7 +256,7 @@
         ],
         compiler_params=params(12),
         name="select",
-    )(neighbors, atom_slot, pair, *others)
+    )(table, pair, *others)
     side = math.isqrt(ncol)
 
     def stage(k, first):
@@ -281,7 +284,6 @@
         in_specs=[pl.BlockSpec(line.shape, lambda p: (0, 0))] * side
         + [
             SMEM,
-            SMEM,
             pl.BlockSpec((1, WIDTH, WIDTH), lambda p: (p, 0, 0)),
         ],
         out_specs=pl.BlockSpec((ncol * PANEL, LANES), lambda p: (0, 0)),
@@ -293,12 +295,12 @@
         ],
         compiler_params=params(48),
         name="exchange",
-    )(*plane, neighbors, atom_slot, tensor)
+    )(*plane, table, tensor)
     parts = lax.all_to_all(sent.reshape(ncol, PANEL, LANES), "col", 0, 0, tiled=True)
     mine, other = pl.pallas_call(
         functools.partial(place_kernel, ny, ncol, rows),
         out_shape=[jax.ShapeDtypeStruct((ny, rows, cols), jnp.float32)] * 2,
-        in_specs=[SMEM, SMEM, VMEM],
+        in_specs=[SMEM, VMEM],
         out_specs=[VMEM, VMEM],
         scratch_shapes=[
             pltpu.VMEM((PANEL, LANES), jnp.float32),
@@ -307,7 +309,7 @@
         ],
         compiler_params=params(12),
         name="place",
-    )(neighbors, atom_slot, parts)
+    )(table, parts)
     chip = mine + lax.ppermute(other, "row", core)
     direct = chip[0]
     for k in range(1, ny):

time: 122 us -> 118 us (0.967)
  local copies, waits for them, and re-layouts: 3.45 us -> 0.83 us
  Pallas kernels: 31 us -> 29.2 us
    unnamed x9 -> x1, local copies, waits for them, and re-layouts: 3.42 us -> 0.8 us
    pallas_call x1, Pallas kernels: 27.5 us -> 25.9 us  [shards(): pl.pallas_call(functools.partial(exchange_kernel, side), out_shape=jax.Sh...]
  transfers between devices with their start and end apart: 16 -> 16, of which waited for: 13 -> 12; matrix products, arithmetic and copies ran while one was open for 1% -> 1% of each run, Pallas kernels for 0% -> 0%
where the time goes in v4:
time: 118 us
  starting transfers between devices  32.6 us (28%)
  waiting for transfers between devices  29.5 us (25%)
  Pallas kernels  29.2 us (25%)
  blocking collectives  24.8 us (21%)
    pallas_call x1, Pallas kernels, shards(): pl.pallas_call(functools.partial(exchange_kernel, side), out_shape=jax.Sh...  25.9 us
    all_to_all x1, blocking collectives, shards(): lax.all_to_all(sent.reshape(ncol, PANEL, LANES), 'col', 0, 0, tiled=True)  24.8 us
    ppermute x3, waiting for transfers between devices, shards(): lax.ppermute(line, both, stage(k, False))  9.57 us
    ppermute x1, starting transfers between devices, shards(): first = lax.ppermute(jnp.where(b == 0, upper, lower), ('row', 'col'), same)  7.57 us
    ppermute x1, waiting for transfers between devices, shards(): second = lax.ppermute(jnp.where(b == 0, lower, upper), ('row', 'col'), swap)  5.63 us
    ppermute x1, starting transfers between devices, shards(): chip = mine + lax.ppermute(other, 'row', core)  5.39 us
    ppermute x3, starting transfers between devices, shards(): others = [lax.ppermute(pair, 'row', along(k)) for k in range(1, ny)]  5.05 us
    ppermute x3, starting transfers between devices, shards(): lax.ppermute(line, both, stage(k, False))  4.76 us
  transfers between devices with their start and end apart: 16, of which 12 were waited for; matrix products, arithmetic and copies ran while one was open for 1% of the time, Pallas kernels for 0%

profile of v4, /device:TPU:65, one launch (start us, length us, event | category | flops | bytes accessed | tf_op | source)
XLA Modules:
  0.0 117.9 jit_solution(14260089288838666797)
XLA Ops:
  1.8 1.4 %collective-permute-start.1 = (bf16[384,96]{1,0:T(8,128)(2,1)S(1)}, bf16[384,96]{1,0:T(8,128)(2,1)S(1)}, u32[]{:S(2)}, u32[]{:S(2)}) collective-permute-start(bf16[384,96]{1,0:T(8,128)(2,1)S(1)} %constant_dynamic-update-slice_fusion.p0), channel_id=1, source_target_pairs={{0,32},{16,48},{32,64},{48,80},{64,96},{80,112},{96,0},{112,16},{1... | collective-permute-start | bytes 221192 | tf_op jit(solution)/shard_map/ppermute | solution.py:245
  3.1 2.6 %collective-permute-start.2 = (bf16[384,96]{1,0:T(8,128)(2,1)S(1)}, bf16[384,96]{1,0:T(8,128)(2,1)S(1)}, u32[]{:S(2)}, u32[]{:S(2)}) collective-permute-start(bf16[384,96]{1,0:T(8,128)(2,1)S(1)} %constant_dynamic-update-slice_fusion.p0), channel_id=1, source_target_pairs={{0,64},{16,80},{32,96},{48,112},{64,0},{80,16},{96,32},{112,48},{1... | collective-permute-start | bytes 221192 | tf_op jit(solution)/shard_map/ppermute | solution.py:245
  5.8 1.1 collective-permute-start.3
  7.6 2.8 %collective-permute-done.2.p2 = bf16[384,96]{1,0:T(8,128)(2,1)S(1)} collective-permute-done((bf16[384,96]{1,0:T(8,128)(2,1)S(1)}, bf16[384,96]{1,0:T(8,128)(2,1)S(1)}, u32[]{:S(2)}, u32[]{:S(2)}) %collective-permute-start.2) | collective-permute-done | bytes 73760 | tf_op jit(solution)/shard_map/ppermute | solution.py:245
  10.4 1.5 %select.3 = bf16[432,128]{1,0:T(8,128)(2,1)S(1)} custom-call(s32[80]{0:T(128)S(1)} %pad_add_fusion.table, bf16[384,96]{1,0:T(8,128)(2,1)S(1)} %constant_dynamic-update-slice_fusion.p0, bf16[384,96]{1,0:T(8,128)(2,1)S(1)} %collective-permute-done.1.p1, bf16[384,96]{1,0:T(8,128)(2,1)S(1)} %collective-permute-done.2.p2, ...), custom_call_target="tpu_custom_call" | custom-call | tf_op jit(solution)/shard_map/select/pallas_call | solution.py:246
  11.9 1.4 %collective-permute-start.4 = (bf16[432,128]{1,0:T(8,128)(2,1)S(1)}, bf16[432,128]{1,0:T(8,128)(2,1)S(1)}, u32[]{:S(2)}, u32[]{:S(2)}) collective-permute-start(bf16[432,128]{1,0:T(8,128)(2,1)S(1)} %select.3), channel_id=1, source_target_pairs={{0,1},{1,2},{2,3},{3,0},{4,5},{5,6},{6,7},{7,4},{8,9},{9,10},{10,1... | collective-permute-start | bytes 331784 | tf_op jit(solution)/shard_map/ppermute | solution.py:275
  13.3 1.3 %collective-permute-start.6 = (bf16[432,128]{1,0:T(8,128)(2,1)S(1)}, bf16[432,128]{1,0:T(8,128)(2,1)S(1)}, u32[]{:S(2)}, u32[]{:S(2)}) collective-permute-start(bf16[432,128]{1,0:T(8,128)(2,1)S(1)} %select.3), channel_id=1, source_target_pairs={{0,3},{1,0},{2,1},{3,2},{4,7},{5,4},{6,5},{7,6},{8,11},{9,8},{10,9... | collective-permute-start | bytes 331784 | tf_op jit(solution)/shard_map/ppermute | solution.py:275
  15.6 3.1 %collective-permute-done.5 = bf16[432,128]{1,0:T(8,128)(2,1)S(1)} collective-permute-done((bf16[432,128]{1,0:T(8,128)(2,1)S(1)}, bf16[432,128]{1,0:T(8,128)(2,1)S(1)}, u32[]{:S(2)}, u32[]{:S(2)}) %collective-permute-start.5) | collective-permute-done | bytes 110624 | tf_op jit(solution)/shard_map/ppermute | solution.py:275
  18.8 1.2 collective-permute-start.7
  19.9 2.7 %collective-permute-start.8 = (bf16[1728,128]{1,0:T(8,128)(2,1)S(1)}, bf16[1728,128]{1,0:T(8,128)(2,1)S(1)}, u32[]{:S(2)}, u32[]{:S(2)}) collective-permute-start(bf16[1728,128]{1,0:T(8,128)(2,1)S(1)} %pad_maximum_fusion.q0), channel_id=1, source_target_pairs={{0,8},{1,9},{2,10},{3,11},{4,12},{5,13},{6,14},{7,15},{8,0},{9,1},... | collective-permute-start | bytes 1327112 | tf_op jit(solution)/shard_map/ppermute | solution.py:277
  23.5 3.7 %collective-permute-done.7.q1 = bf16[1728,128]{1,0:T(8,128)(2,1)S(1)} collective-permute-done((bf16[1728,128]{1,0:T(8,128)(2,1)S(1)}, bf16[1728,128]{1,0:T(8,128)(2,1)S(1)}, u32[]{:S(2)}, u32[]{:S(2)}) %collective-permute-start.7) | collective-permute-done | bytes 442400 | tf_op jit(solution)/shard_map/ppermute | solution.py:277
  27.2 5.9 %collective-permute-done.8.q2 = bf16[1728,128]{1,0:T(8,128)(2,1)S(1)} collective-permute-done((bf16[1728,128]{1,0:T(8,128)(2,1)S(1)}, bf16[1728,128]{1,0:T(8,128)(2,1)S(1)}, u32[]{:S(2)}, u32[]{:S(2)}) %collective-permute-start.8) | collective-permute-done | bytes 442400 | tf_op jit(solution)/shard_map/ppermute | solution.py:277
  33.1 25.9 %exchange.1 = bf16[6912,128]{1,0:T(8,128)(2,1)S(1)} custom-call(bf16[1728,128]{1,0:T(8,128)(2,1)S(1)} %pad_maximum_fusion.q0, bf16[1728,128]{1,0:T(8,128)(2,1)S(1)} %collective-permute-done.7.q1, bf16[1728,128]{1,0:T(8,128)(2,1)S(1)} %collective-permute-done.8.q2, bf16[1728,128]{1,0:T(8,128)(2,1)S(1)} %collective-permute-done.9.q3, ...), custom_call_target="tpu_custom_call" | custom-call | tf_op jit(solution)/shard_map/exchange/pallas_call | solution.py:280
  59.0 24.8 %all_to_all.5.parts = bf16[16,432,128]{2,1,0:T(8,128)(2,1)S(1)} all-to-all(bf16[16,432,128]{2,1,0:T(8,128)(2,1)S(1)} %bitcast.17), channel_id=1, replica_groups=mesh['row'=8,'col'=16] {'col'}, dimensions={0} | all-to-all | bytes 3538944 | tf_op jit(solution)/shard_map/all_to_all | solution.py:299
  83.7 1.2 place.1
  84.9 5.4 %collective-permute-start.10 = (f32[4,192,96]{2,1,0:T(8,128)S(1)}, f32[4,192,96]{2,1,0:T(8,128)S(1)}, u32[]{:S(2)}, u32[]{:S(2)}) collective-permute-start(f32[4,192,96]{2,1,0:T(8,128)S(1)} %get-tuple-element.8), channel_id=1, source_target_pairs={{0,16},{16,0},{32,48},{48,32},{64,80},{80,64},{96,112},{112,96},{1... | collective-permute-start | bytes 884744 | tf_op jit(solution)/shard_map/ppermute | solution.py:313
  90.3 1.3 %collective-permute-done.10 = f32[4,192,96]{2,1,0:T(8,128)S(1)} collective-permute-done((f32[4,192,96]{2,1,0:T(8,128)S(1)}, f32[4,192,96]{2,1,0:T(8,128)S(1)}, u32[]{:S(2)}, u32[]{:S(2)}) %collective-permute-start.10) | collective-permute-done | bytes 294944 | tf_op jit(solution)/shard_map/ppermute | solution.py:313
  92.6 2.1 %collective-permute-start.12 = (f32[192,96]{1,0:T(8,128)S(1)}, f32[192,96]{1,0:T(8,128)S(1)}, u32[]{:S(2)}, u32[]{:S(2)}) collective-permute-start(f32[192,96]{1,0:T(8,128)S(1)} %get-tuple-element.11), channel_id=1, source_target_pairs={{0,64},{16,80},{32,96},{48,112},{64,0},{80,16},{96,32},{112,48},{1... | collective-permute-start | bytes 221192 | tf_op jit(solution)/shard_map/ppermute | solution.py:316
  94.7 1.4 %collective-permute-start.13 = (f32[192,96]{1,0:T(8,128)S(1)}, f32[192,96]{1,0:T(8,128)S(1)}, u32[]{:S(2)}, u32[]{:S(2)}) collective-permute-start(f32[192,96]{1,0:T(8,128)S(1)} %get-tuple-element.10), channel_id=1, source_target_pairs={{0,96},{16,112},{32,0},{48,16},{64,32},{80,48},{96,64},{112,80},{1... | collective-permute-start | bytes 221192 | tf_op jit(solution)/shard_map/ppermute | solution.py:316
  97.0 2.3 %collective-permute-done.12 = f32[192,96]{1,0:T(8,128)S(1)} collective-permute-done((f32[192,96]{1,0:T(8,128)S(1)}, f32[192,96]{1,0:T(8,128)S(1)}, u32[]{:S(2)}, u32[]{:S(2)}) %collective-permute-start.12) | collective-permute-done | bytes 73760 | tf_op jit(solution)/shard_map/ppermute | solution.py:316
  99.6 7.6 %collective-permute-start.14 = (f32[96,96]{1,0:T(8,128)S(1)}, f32[96,96]{1,0:T(8,128)S(1)}, u32[]{:S(2)}, u32[]{:S(2)}) collective-permute-start(f32[96,96]{1,0:T(8,128)S(1)} %get-tuple-element.13), channel_id=1, source_target_pairs={{0,0},{1,1},{2,16},{3,17},{4,32},{5,33},{6,48},{7,49},{8,64},{9,65... | collective-permute-start | bytes 110600 | tf_op jit(solution)/shard_map/ppermute | solution.py:322
  107.1 2.1 %collective-permute-start.15 = (f32[96,96]{1,0:T(8,128)S(1)}, f32[96,96]{1,0:T(8,128)S(1)}, u32[]{:S(2)}, u32[]{:S(2)}) collective-permute-start(f32[96,96]{1,0:T(8,128)S(1)} %get-tuple-element.12), channel_id=1, source_target_pairs={{0,1},{1,0},{2,17},{3,16},{4,33},{5,32},{6,49},{7,48},{8,65},{9,64... | collective-permute-start | bytes 110600 | tf_op jit(solution)/shard_map/ppermute | solution.py:323
  109.3 2.2 %collective-permute-done.14.first = f32[96,96]{1,0:T(8,128)S(1)} collective-permute-done((f32[96,96]{1,0:T(8,128)S(1)}, f32[96,96]{1,0:T(8,128)S(1)}, u32[]{:S(2)}, u32[]{:S(2)}) %collective-permute-start.14) | collective-permute-done | bytes 36896 | tf_op jit(solution)/shard_map/ppermute | solution.py:322
  111.5 5.6 %collective-permute-done.15.second = f32[96,96]{1,0:T(8,128)S(1)} collective-permute-done((f32[96,96]{1,0:T(8,128)S(1)}, f32[96,96]{1,0:T(8,128)S(1)}, u32[]{:S(2)}, u32[]{:S(2)}) %collective-permute-start.15) | collective-permute-done | bytes 36896 | tf_op jit(solution)/shard_map/ppermute | solution.py:323
  (21 shorter events, 7.2 us)
Async XLA Ops:
  0.0 1.8 %collective-permute-start = (bf16[192,96]{1,0:T(8,128)(2,1)}, bf16[192,96]{1,0:T(8,128)(2,1)S(1)}, u32[]{:S(2)}, u32[]{:S(2)}) collective-permute-start(bf16[192,96]{1,0:T(8,128)(2,1)} %param.5), channel_id=1, source_target_pairs={{0,16},{16,0},{32,48},{48,32},{64,80},{80,64},{96,112},{112,96},{1... | collective-permute-start | bytes 110600 | tf_op jit(solution)/shard_map/ppermute | solution.py:244
  1.8 5.8 %collective-permute-start.1 = (bf16[384,96]{1,0:T(8,128)(2,1)S(1)}, bf16[384,96]{1,0:T(8,128)(2,1)S(1)}, u32[]{:S(2)}, u32[]{:S(2)}) collective-permute-start(bf16[384,96]{1,0:T(8,128)(2,1)S(1)} %constant_dynamic-update-slice_fusion.p0), channel_id=1, source_target_pairs={{0,32},{16,48},{32,64},{48,80},{64,96},{80,112},{96,0},{112,16},{1... | collective-permute-start | bytes 221192 | tf_op jit(solution)/shard_map/ppermute | solution.py:245
  3.1 7.3 %collective-permute-start.2 = (bf16[384,96]{1,0:T(8,128)(2,1)S(1)}, bf16[384,96]{1,0:T(8,128)(2,1)S(1)}, u32[]{:S(2)}, u32[]{:S(2)}) collective-permute-start(bf16[384,96]{1,0:T(8,128)(2,1)S(1)} %constant_dynamic-update-slice_fusion.p0), channel_id=1, source_target_pairs={{0,64},{16,80},{32,96},{48,112},{64,0},{80,16},{96,32},{112,48},{1... | collective-permute-start | bytes 221192 | tf_op jit(solution)/shard_map/ppermute | solution.py:245
  5.8 4.7 %collective-permute-start.3 = (bf16[384,96]{1,0:T(8,128)(2,1)S(1)}, bf16[384,96]{1,0:T(8,128)(2,1)S(1)}, u32[]{:S(2)}, u32[]{:S(2)}) collective-permute-start(bf16[384,96]{1,0:T(8,128)(2,1)S(1)} %constant_dynamic-update-slice_fusion.p0), channel_id=1, source_target_pairs={{0,96},{16,112},{32,0},{48,16},{64,32},{80,48},{96,64},{112,80},{1... | collective-permute-start | bytes 221192 | tf_op jit(solution)/shard_map/ppermute | solution.py:245
  11.9 3.7 %collective-permute-start.4 = (bf16[432,128]{1,0:T(8,128)(2,1)S(1)}, bf16[432,128]{1,0:T(8,128)(2,1)S(1)}, u32[]{:S(2)}, u32[]{:S(2)}) collective-permute-start(bf16[432,128]{1,0:T(8,128)(2,1)S(1)} %select.3), channel_id=1, source_target_pairs={{0,1},{1,2},{2,3},{3,0},{4,5},{5,6},{6,7},{7,4},{8,9},{9,10},{10,1... | collective-permute-start | bytes 331784 | tf_op jit(solution)/shard_map/ppermute | solution.py:275
  13.3 5.4 %collective-permute-start.5 = (bf16[432,128]{1,0:T(8,128)(2,1)S(1)}, bf16[432,128]{1,0:T(8,128)(2,1)S(1)}, u32[]{:S(2)}, u32[]{:S(2)}) collective-permute-start(bf16[432,128]{1,0:T(8,128)(2,1)S(1)} %select.3), channel_id=1, source_target_pairs={{0,2},{1,3},{2,0},{3,1},{4,6},{5,7},{6,4},{7,5},{8,10},{9,11},{10,... | collective-permute-start | bytes 331784 | tf_op jit(solution)/shard_map/ppermute | solution.py:275
  13.3 5.4 %collective-permute-start.6 = (bf16[432,128]{1,0:T(8,128)(2,1)S(1)}, bf16[432,128]{1,0:T(8,128)(2,1)S(1)}, u32[]{:S(2)}, u32[]{:S(2)}) collective-permute-start(bf16[432,128]{1,0:T(8,128)(2,1)S(1)} %select.3), channel_id=1, source_target_pairs={{0,3},{1,0},{2,1},{3,2},{4,7},{5,4},{6,5},{7,6},{8,11},{9,8},{10,9... | collective-permute-start | bytes 331784 | tf_op jit(solution)/shard_map/ppermute | solution.py:275
  18.8 8.4 %collective-permute-start.7 = (bf16[1728,128]{1,0:T(8,128)(2,1)S(1)}, bf16[1728,128]{1,0:T(8,128)(2,1)S(1)}, u32[]{:S(2)}, u32[]{:S(2)}) collective-permute-start(bf16[1728,128]{1,0:T(8,128)(2,1)S(1)} %pad_maximum_fusion.q0), channel_id=1, source_target_pairs={{0,4},{1,5},{2,6},{3,7},{4,8},{5,9},{6,10},{7,11},{8,12},{9,13},{1... | collective-permute-start | bytes 1327112 | tf_op jit(solution)/shard_map/ppermute | solution.py:277
  19.9 13.2 %collective-permute-start.8 = (bf16[1728,128]{1,0:T(8,128)(2,1)S(1)}, bf16[1728,128]{1,0:T(8,128)(2,1)S(1)}, u32[]{:S(2)}, u32[]{:S(2)}) collective-permute-start(bf16[1728,128]{1,0:T(8,128)(2,1)S(1)} %pad_maximum_fusion.q0), channel_id=1, source_target_pairs={{0,8},{1,9},{2,10},{3,11},{4,12},{5,13},{6,14},{7,15},{8,0},{9,1},... | collective-permute-start | bytes 1327112 | tf_op jit(solution)/shard_map/ppermute | solution.py:277
  22.7 10.4 %collective-permute-start.9 = (bf16[1728,128]{1,0:T(8,128)(2,1)S(1)}, bf16[1728,128]{1,0:T(8,128)(2,1)S(1)}, u32[]{:S(2)}, u32[]{:S(2)}) collective-permute-start(bf16[1728,128]{1,0:T(8,128)(2,1)S(1)} %pad_maximum_fusion.q0), channel_id=1, source_target_pairs={{0,12},{1,13},{2,14},{3,15},{4,0},{5,1},{6,2},{7,3},{8,4},{9,5},{1... | collective-permute-start | bytes 1327112 | tf_op jit(solution)/shard_map/ppermute | solution.py:277
  84.9 6.7 %collective-permute-start.10 = (f32[4,192,96]{2,1,0:T(8,128)S(1)}, f32[4,192,96]{2,1,0:T(8,128)S(1)}, u32[]{:S(2)}, u32[]{:S(2)}) collective-permute-start(f32[4,192,96]{2,1,0:T(8,128)S(1)} %get-tuple-element.8), channel_id=1, source_target_pairs={{0,16},{16,0},{32,48},{48,32},{64,80},{80,64},{96,112},{112,96},{1... | collective-permute-start | bytes 884744 | tf_op jit(solution)/shard_map/ppermute | solution.py:313
  91.7 5.3 %collective-permute-start.11 = (f32[192,96]{1,0:T(8,128)S(1)}, f32[192,96]{1,0:T(8,128)S(1)}, u32[]{:S(2)}, u32[]{:S(2)}) collective-permute-start(f32[192,96]{1,0:T(8,128)S(1)} %get-tuple-element.9), channel_id=1, source_target_pairs={{0,32},{16,48},{32,64},{48,80},{64,96},{80,112},{96,0},{112,16},{1... | collective-permute-start | bytes 221192 | tf_op jit(solution)/shard_map/ppermute | solution.py:316
  92.6 6.8 %collective-permute-start.12 = (f32[192,96]{1,0:T(8,128)S(1)}, f32[192,96]{1,0:T(8,128)S(1)}, u32[]{:S(2)}, u32[]{:S(2)}) collective-permute-start(f32[192,96]{1,0:T(8,128)S(1)} %get-tuple-element.11), channel_id=1, source_target_pairs={{0,64},{16,80},{32,96},{48,112},{64,0},{80,16},{96,32},{112,48},{1... | collective-permute-start | bytes 221192 | tf_op jit(solution)/shard_map/ppermute | solution.py:316
  94.7 4.8 %collective-permute-start.13 = (f32[192,96]{1,0:T(8,128)S(1)}, f32[192,96]{1,0:T(8,128)S(1)}, u32[]{:S(2)}, u32[]{:S(2)}) collective-permute-start(f32[192,96]{1,0:T(8,128)S(1)} %get-tuple-element.10), channel_id=1, source_target_pairs={{0,96},{16,112},{32,0},{48,16},{64,32},{80,48},{96,64},{112,80},{1... | collective-permute-start | bytes 221192 | tf_op jit(solution)/shard_map/ppermute | solution.py:316
  99.6 12.0 %collective-permute-start.14 = (f32[96,96]{1,0:T(8,128)S(1)}, f32[96,96]{1,0:T(8,128)S(1)}, u32[]{:S(2)}, u32[]{:S(2)}) collective-permute-start(f32[96,96]{1,0:T(8,128)S(1)} %get-tuple-element.13), channel_id=1, source_target_pairs={{0,0},{1,1},{2,16},{3,17},{4,32},{5,33},{6,48},{7,49},{8,64},{9,65... | collective-permute-start | bytes 110600 | tf_op jit(solution)/shard_map/ppermute | solution.py:322
  107.1 10.0 %collective-permute-start.15 = (f32[96,96]{1,0:T(8,128)S(1)}, f32[96,96]{1,0:T(8,128)S(1)}, u32[]{:S(2)}, u32[]{:S(2)}) collective-permute-start(f32[96,96]{1,0:T(8,128)S(1)} %get-tuple-element.12), channel_id=1, source_target_pairs={{0,1},{1,0},{2,17},{3,16},{4,33},{5,32},{6,49},{7,48},{8,65},{9,64... | collective-permute-start | bytes 110600 | tf_op jit(solution)/shard_map/ppermute | solution.py:323

commit v5 on v4

--- a/solution.py
+++ b/solution.py
@@ -58,7 +58,7 @@
     col = lax.axis_index("col")
     y, h = row // 2, row % 2
     copies = []
-    for shift, part in enumerate((p0, p1, p2, p3)):
+    for shift, part in zip((0,) + SHIFTS, (p0, p1, p2, p3)):
         owner = lax.rem(y - shift + ny, ny)
         for side in range(2):
             at = pl.multiple_of((2 * owner + (h if side == 0 else 1 - h)) * rows, 32)
@@ -98,84 +98,96 @@
     return (storage // 3) * PANEL, storage % 3
 
 
-def exchange_kernel(side, q0, q1, q2, q3, table, tensor, out, gathered, local, half, acc):
-    step = pl.program_id(0)
+def exchange_kernel(side, q0, q1, q2, q3, table, tensor, out, gathered, local, half, acc, fetched, sem):
+    nfun = tensor.shape[0]
     big = 2 * LANES
     tiles = WIDTH // big
 
-    @pl.when(step == 0)
-    def _():
-        h = lax.axis_index("row") % 2
-        z, x = lax.axis_index("col") // side, lax.axis_index("col") % side
-        left = lax.broadcasted_iota(jnp.int32, (BS, LANES), 1) < LANES // 2
-        for j, part in enumerate((q0, q1, q2, q3)):
-            for k in range(side):
-                dz, dx = jnp.where(h == 0, j, k), jnp.where(h == 0, k, j)
-                owner = lax.rem(z - dz + side, side) * side + lax.rem(x - dx + side, side)
-                at = pl.multiple_of(owner * PANEL, 16)
-                gathered[pl.ds(at, PANEL), :] = part[k * PANEL : (k + 1) * PANEL, :]
-        for k in range(KN):
-            base, j = place_of(table[KN + table[k]])
-            group = k // GB
-            for d in range(ND - 1):
-                to = (group + d) % NG
-                at = pl.multiple_of(base + (d * 3 + j) * BS, 16)
-                local[k * BS : (k + 1) * BS, to * LANES : (to + 1) * LANES] = gathered[pl.ds(at, BS), :]
-            at = pl.multiple_of(base + TAIL + j * HB, 16)
-            tile = unpack_far(gathered[pl.ds(at, HB), :].astype(jnp.float32))
-            if far_half(k):
-                tile = jnp.where(left, 0.0, pltpu.roll(tile, LANES // 2, 1))
-            else:
-                tile = jnp.where(left, tile, 0.0)
-            to = (group + NG // 2) % NG
-            local[k * BS : (k + 1) * BS, to * LANES : (to + 1) * LANES] = tile.astype(jnp.bfloat16)
-        for group in range(NG):
-            here = slice(group * LANES, (group + 1) * LANES)
-            for d in range(1, NG // 2):
-                to = (group + d) % NG
-                there = slice(to * LANES, (to + 1) * LANES)
-                local[there, here] = local[here, there].T
-        for group in range(NG // 2):
-            here = slice(group * LANES, (group + 1) * LANES)
-            there = slice((group + NG // 2) * LANES, (group + NG // 2 + 1) * LANES)
-            tile = local[here, there] + local[there, here].T
-            local[here, there] = tile
-            local[there, here] = tile.T
-        acc[...] = jnp.zeros_like(acc)
-
-    for i in range(tiles):
-        half[i * big : (i + 1) * big, :] = jnp.dot(
-            local[i * big : (i + 1) * big, :], tensor[0], preferred_element_type=jnp.float32
+    def fetch(p):
+        return pltpu.make_async_copy(tensor.at[p], fetched.at[p % 3], sem.at[p])
+
+    def first_product(p):
+        half[p % 2] = jnp.dot(
+            local[...], fetched[p % 3], preferred_element_type=jnp.float32
         ).astype(jnp.bfloat16)
-    for i in range(tiles):
-        left = tensor[0, i * big : (i + 1) * big, :]
-        first, second = ((tiles - 1, 0), (tiles - 1, 0), (2, 0), (1, 1))[i]
-        acc[i, :, : first * big] += jnp.dot(
-            left, half[:, i * big : (i + first) * big], preferred_element_type=jnp.float32
-        )
-        if second:
-            acc[i, :, first * big : (first + second) * big] += jnp.dot(
-                left, half[:, : second * big], preferred_element_type=jnp.float32
+
+    def second_product(p):
+        for i in range(tiles):
+            left = fetched[p % 3, i * big : (i + 1) * big, :]
+            first, second = ((tiles - 1, 0), (tiles - 1, 0), (2, 0), (1, 1))[i]
+            acc[i, :, : first * big] += jnp.dot(
+                left, half[p % 2, :, i * big : (i + first) * big], preferred_element_type=jnp.float32
             )
-
-    @pl.when(step == pl.num_programs(0) - 1)
-    def _():
-        ncol = lax.axis_size("col")
-        scale = 1.0 + lax.axis_index("col").astype(jnp.float32) / ncol
-        out[...] = jnp.zeros_like(out)
-        for i in range(tiles // 2):
-            acc[i + tiles // 2, :, 2 * big :] = acc[i, :, 2 * big :].T
-        for k in range(KN):
-            base, j = place_of(table[KN + table[k]])
-            group = k // GB
-            i, odd = group // 2, group % 2
-            r = (k % (2 * GB)) * BS
-            piece = acc[i, r : r + BS, odd * LANES : odd * LANES + KEEP] * scale
-            for d in range(ND - 1):
-                at = pl.multiple_of(base + (d * 3 + j) * BS, 16)
-                out[pl.ds(at, BS), :] = piece[:, d * LANES : (d + 1) * LANES].astype(jnp.bfloat16)
-            at = pl.multiple_of(base + TAIL + j * HB, 16)
-            out[pl.ds(at, HB), :] = pack_far(piece[:, FAR:], far_half(k)).astype(jnp.bfloat16)
+            if second:
+                acc[i, :, first * big : (first + second) * big] += jnp.dot(
+                    left, half[p % 2, :, : second * big], preferred_element_type=jnp.float32
+                )
+
+    fetch(0).start()
+    h = lax.axis_index("row") % 2
+    z, x = lax.axis_index("col") // side, lax.axis_index("col") % side
+    left = lax.broadcasted_iota(jnp.int32, (BS, LANES), 1) < LANES // 2
+    for j, part in zip((0,) + SHIFTS, (q0, q1, q2, q3)):
+        for i, k in enumerate((0,) + SHIFTS):
+            dz, dx = jnp.where(h == 0, j, k), jnp.where(h == 0, k, j)
+            owner = lax.rem(z - dz + side, side) * side + lax.rem(x - dx + side, side)
+            at = pl.multiple_of(owner * PANEL, 16)
+            gathered[pl.ds(at, PANEL), :] = part[i * PANEL : (i + 1) * PANEL, :]
+    for k in range(KN):
+        base, j = place_of(table[KN + table[k]])
+        group = k // GB
+        for d in range(ND - 1):
+            to = (group + d) % NG
+            at = pl.multiple_of(base + (d * 3 + j) * BS, 16)
+            local[k * BS : (k + 1) * BS, to * LANES : (to + 1) * LANES] = gathered[pl.ds(at, BS), :]
+        at = pl.multiple_of(base + TAIL + j * HB, 16)
+        tile = unpack_far(gathered[pl.ds(at, HB), :].astype(jnp.float32))
+        if far_half(k):
+            tile = jnp.where(left, 0.0, pltpu.roll(tile, LANES // 2, 1))
+        else:
+            tile = jnp.where(left, tile, 0.0)
+        to = (group + NG // 2) % NG
+        local[k * BS : (k + 1) * BS, to * LANES : (to + 1) * LANES] = tile.astype(jnp.bfloat16)
+    for group in range(NG):
+        here = slice(group * LANES, (group + 1) * LANES)
+        for d in range(1, NG // 2):
+            to = (group + d) % NG
+            there = slice(to * LANES, (to + 1) * LANES)
+            local[there, here] = local[here, there].T
+    for group in range(NG // 2):
+        here = slice(group * LANES, (group + 1) * LANES)
+        there = slice((group + NG // 2) * LANES, (group + NG // 2 + 1) * LANES)
+        tile = local[here, there] + local[there, here].T
+        local[here, there] = tile
+        local[there, here] = tile.T
+    acc[...] = jnp.zeros_like(acc)
+    fetch(1).start()
+    fetch(0).wait()
+    first_product(0)
+    for p in range(nfun):
+        if p + 2 < nfun:
+            fetch(p + 2).start()
+        if p + 1 < nfun:
+            fetch(p + 1).wait()
+            first_product(p + 1)
+        second_product(p)
+
+    ncol = lax.axis_size("col")
+    scale = 1.0 + lax.axis_index("col").astype(jnp.float32) / ncol
+    out[...] = jnp.zeros_like(out)
+    for i in range(tiles // 2):
+        acc[i + tiles // 2, :, 2 * big :] = acc[i, :, 2 * big :].T
+    for k in range(KN):
+        base, j = place_of(table[KN + table[k]])
+        group = k // GB
+        i, odd = group // 2, group % 2
+        r = (k % (2 * GB)) * BS
+        piece = acc[i, r : r + BS, odd * LANES : odd * LANES + KEEP] * scale
+        for d in range(ND - 1):
+            at = pl.multiple_of(base + (d * 3 + j) * BS, 16)
+            out[pl.ds(at, BS), :] = piece[:, d * LANES : (d + 1) * LANES].astype(jnp.bfloat16)
+        at = pl.multiple_of(base + TAIL + j * HB, 16)
+        out[pl.ds(at, HB), :] = pack_far(piece[:, FAR:], far_half(k)).astype(jnp.bfloat16)
 
 
 def place_kernel(ny, ncol, rows, table, parts, mine, other, total, turned, placed):
@@ -224,6 +236,9 @@
         out[pl.ds(at, part), :] = direct[pl.ds(at, part), :] + block[...].T
 
 
+SHIFTS = (2, 1, 3)
+
+
 VMEM = pl.BlockSpec(memory_space=pltpu.VMEM)
 SMEM = pl.BlockSpec(memory_space=pltpu.SMEM)
 ANY = pl.BlockSpec(memory_space=pl.ANY)
@@ -242,7 +257,7 @@
 
     table = jnp.concatenate([neighbors[0], atom_slot])
     pair = jnp.concatenate([density, lax.ppermute(density, "row", core)], axis=0)
-    others = [lax.ppermute(pair, "row", along(k)) for k in range(1, ny)]
+    others = [lax.ppermute(pair, "row", along(k)) for k in SHIFTS]
     block = pl.pallas_call(
         functools.partial(select_kernel, ny, ncol, rows),
         out_shape=jax.ShapeDtypeStruct((PANEL, LANES), jnp.bfloat16),
@@ -272,26 +287,23 @@
         return pairs
 
     both = ("row", "col")
-    line = [block] + [lax.ppermute(block, both, stage(k, True)) for k in range(1, side)]
+    line = [block] + [lax.ppermute(block, both, stage(k, True)) for k in SHIFTS]
     line = jnp.concatenate(line, axis=0)
-    plane = [line] + [lax.ppermute(line, both, stage(k, False)) for k in range(1, side)]
+    plane = [line] + [lax.ppermute(line, both, stage(k, False)) for k in SHIFTS]
     tensor = three_center[0]
     nfun = tensor.shape[0]
     sent = pl.pallas_call(
         functools.partial(exchange_kernel, side),
         out_shape=jax.ShapeDtypeStruct((ncol * PANEL, LANES), jnp.bfloat16),
-        grid=(nfun,),
-        in_specs=[pl.BlockSpec(line.shape, lambda p: (0, 0))] * side
-        + [
-            SMEM,
-            pl.BlockSpec((1, WIDTH, WIDTH), lambda p: (p, 0, 0)),
-        ],
-        out_specs=pl.BlockSpec((ncol * PANEL, LANES), lambda p: (0, 0)),
+        in_specs=[VMEM] * side + [SMEM, ANY],
+        out_specs=VMEM,
         scratch_shapes=[
             pltpu.VMEM((ncol * PANEL, LANES), jnp.bfloat16),
             pltpu.VMEM((WIDTH, WIDTH), jnp.bfloat16),
-            pltpu.VMEM((WIDTH, WIDTH), jnp.bfloat16),
+            pltpu.VMEM((2, WIDTH, WIDTH), jnp.bfloat16),
             pltpu.VMEM((4, 2 * LANES, 6 * LANES), jnp.float32),
+            pltpu.VMEM((3, WIDTH, WIDTH), jnp.bfloat16),
+            pltpu.SemaphoreType.DMA((nfun,)),
         ],
         compiler_params=params(48),
         name="exchange",
@@ -312,7 +324,7 @@
     )(table, parts)
     chip = mine + lax.ppermute(other, "row", core)
     direct = chip[0]
-    for k in range(1, ny):
+    for k in SHIFTS:
         direct = direct + lax.ppermute(chip[k], "row", along(k))
     half = rows // 2
     b = lax.axis_index("col") % 2

time: 118 us -> 117 us (level)
  waiting for transfers between devices: 29.5 us -> 26.5 us
  starting transfers between devices: 32.6 us -> 34.7 us
    ppermute x9, waiting for transfers between devices: 16.5 us -> 13.8 us  [the longest x3 8.4 us: shards(): plane = [line] + [lax.ppermute(line, both, stage(k, False)) for k in SHIFTS]]
    ppermute x9, starting transfers between devices: 12.5 us -> 13.8 us  [the longest x3 5.66 us: shards(): others = [lax.ppermute(pair, 'row', along(k)) for k in SHIFTS]]
  transfers between devices with their start and end apart: 16 -> 16, of which waited for: 12 -> 14; matrix products, arithmetic and copies ran while one was open for 1% -> 1% of each run, Pallas kernels for 0% -> 0%
where the time goes in v5:
time: 117 us
  starting transfers between devices  34.7 us (30%)
  Pallas kernels  29.1 us (25%)
  waiting for transfers between devices  26.5 us (23%)
  blocking collectives  25.2 us (22%)
    pallas_call x1, Pallas kernels, shards(): pl.pallas_call(functools.partial(exchange_kernel, side), out_shape=jax.Sh...  25.7 us
    all_to_all x1, blocking collectives, shards(): lax.all_to_all(sent.reshape(ncol, PANEL, LANES), 'col', 0, 0, tiled=True)  25.2 us
    ppermute x3, waiting for transfers between devices, shards(): plane = [line] + [lax.ppermute(line, both, stage(k, False)) for k in SHIFTS]  8.4 us
    ppermute x1, starting transfers between devices, shards(): first = lax.ppermute(jnp.where(b == 0, upper, lower), ('row', 'col'), same)  7.5 us
    ppermute x1, starting transfers between devices, shards(): chip = mine + lax.ppermute(other, 'row', core)  5.87 us
    ppermute x3, starting transfers between devices, shards(): others = [lax.ppermute(pair, 'row', along(k)) for k in SHIFTS]  5.66 us
    ppermute x3, starting transfers between devices, shards(): plane = [line] + [lax.ppermute(line, both, stage(k, False)) for k in SHIFTS]  5.5 us
    ppermute x1, waiting for transfers between devices, shards(): second = lax.ppermute(jnp.where(b == 0, lower, upper), ('row', 'col'), swap)  5.15 us
  transfers between devices with their start and end apart: 16, of which 14 were waited for; matrix products, arithmetic and copies ran while one was open for 1% of the time, Pallas kernels for 0%

profile of v5, /device:TPU:65, one launch (start us, length us, event | category | flops | bytes accessed | tf_op | source)
XLA Modules:
  0.0 117.2 jit_solution(9812027507326108987)
XLA Ops:
  1.8 3.0 %collective-permute-start.1 = (bf16[384,96]{1,0:T(8,128)(2,1)S(1)}, bf16[384,96]{1,0:T(8,128)(2,1)S(1)}, u32[]{:S(2)}, u32[]{:S(2)}) collective-permute-start(bf16[384,96]{1,0:T(8,128)(2,1)S(1)} %constant_dynamic-update-slice_fusion.p0), channel_id=1, source_target_pairs={{0,64},{16,80},{32,96},{48,112},{64,0},{80,16},{96,32},{112,48},{1... | collective-permute-start | bytes 221192 | tf_op jit(solution)/shard_map/ppermute | solution.py:260
  5.2 2.3 %collective-permute-start.3 = (bf16[384,96]{1,0:T(8,128)(2,1)S(1)}, bf16[384,96]{1,0:T(8,128)(2,1)S(1)}, u32[]{:S(2)}, u32[]{:S(2)}) collective-permute-start(bf16[384,96]{1,0:T(8,128)(2,1)S(1)} %constant_dynamic-update-slice_fusion.p0), channel_id=1, source_target_pairs={{0,96},{16,112},{32,0},{48,16},{64,32},{80,48},{96,64},{112,80},{1... | collective-permute-start | bytes 221192 | tf_op jit(solution)/shard_map/ppermute | solution.py:260
  8.2 1.3 %collective-permute-done.2.p2 = bf16[384,96]{1,0:T(8,128)(2,1)S(1)} collective-permute-done((bf16[384,96]{1,0:T(8,128)(2,1)S(1)}, bf16[384,96]{1,0:T(8,128)(2,1)S(1)}, u32[]{:S(2)}, u32[]{:S(2)}) %collective-permute-start.2) | collective-permute-done | bytes 73760 | tf_op jit(solution)/shard_map/ppermute | solution.py:260
  9.8 1.5 %select.3 = bf16[432,128]{1,0:T(8,128)(2,1)S(1)} custom-call(s32[80]{0:T(128)S(1)} %pad_add_fusion.table, bf16[384,96]{1,0:T(8,128)(2,1)S(1)} %constant_dynamic-update-slice_fusion.p0, bf16[384,96]{1,0:T(8,128)(2,1)S(1)} %collective-permute-done.1.p1, bf16[384,96]{1,0:T(8,128)(2,1)S(1)} %collective-permute-done.2.p2, ...), custom_call_target="tpu_custom_call" | custom-call | tf_op jit(solution)/shard_map/select/pallas_call | solution.py:261
  11.4 1.6 %collective-permute-start.5 = (bf16[432,128]{1,0:T(8,128)(2,1)S(1)}, bf16[432,128]{1,0:T(8,128)(2,1)S(1)}, u32[]{:S(2)}, u32[]{:S(2)}) collective-permute-start(bf16[432,128]{1,0:T(8,128)(2,1)S(1)} %select.3), channel_id=1, source_target_pairs={{0,1},{1,2},{2,3},{3,0},{4,5},{5,6},{6,7},{7,4},{8,9},{9,10},{10,1... | collective-permute-start | bytes 331784 | tf_op jit(solution)/shard_map/ppermute | solution.py:290
  13.9 2.7 %collective-permute-done.4 = bf16[432,128]{1,0:T(8,128)(2,1)S(1)} collective-permute-done((bf16[432,128]{1,0:T(8,128)(2,1)S(1)}, bf16[432,128]{1,0:T(8,128)(2,1)S(1)}, u32[]{:S(2)}, u32[]{:S(2)}) %collective-permute-start.4) | collective-permute-done | bytes 110624 | tf_op jit(solution)/shard_map/ppermute | solution.py:290
  17.7 2.8 %collective-permute-start.7 = (bf16[1728,128]{1,0:T(8,128)(2,1)S(1)}, bf16[1728,128]{1,0:T(8,128)(2,1)S(1)}, u32[]{:S(2)}, u32[]{:S(2)}) collective-permute-start(bf16[1728,128]{1,0:T(8,128)(2,1)S(1)} %pad_maximum_fusion.q0), channel_id=1, source_target_pairs={{0,8},{1,9},{2,10},{3,11},{4,12},{5,13},{6,14},{7,15},{8,0},{9,1},... | collective-permute-start | bytes 1327112 | tf_op jit(solution)/shard_map/ppermute | solution.py:292
  20.9 2.4 %collective-permute-start.9 = (bf16[1728,128]{1,0:T(8,128)(2,1)S(1)}, bf16[1728,128]{1,0:T(8,128)(2,1)S(1)}, u32[]{:S(2)}, u32[]{:S(2)}) collective-permute-start(bf16[1728,128]{1,0:T(8,128)(2,1)S(1)} %pad_maximum_fusion.q0), channel_id=1, source_target_pairs={{0,12},{1,13},{2,14},{3,15},{4,0},{5,1},{6,2},{7,3},{8,4},{9,5},{1... | collective-permute-start | bytes 1327112 | tf_op jit(solution)/shard_map/ppermute | solution.py:292
  23.2 3.3 %collective-permute-done.7.q1 = bf16[1728,128]{1,0:T(8,128)(2,1)S(1)} collective-permute-done((bf16[1728,128]{1,0:T(8,128)(2,1)S(1)}, bf16[1728,128]{1,0:T(8,128)(2,1)S(1)}, u32[]{:S(2)}, u32[]{:S(2)}) %collective-permute-start.7) | collective-permute-done | bytes 442400 | tf_op jit(solution)/shard_map/ppermute | solution.py:292
  26.6 4.8 %collective-permute-done.8.q2 = bf16[1728,128]{1,0:T(8,128)(2,1)S(1)} collective-permute-done((bf16[1728,128]{1,0:T(8,128)(2,1)S(1)}, bf16[1728,128]{1,0:T(8,128)(2,1)S(1)}, u32[]{:S(2)}, u32[]{:S(2)}) %collective-permute-start.8) | collective-permute-done | bytes 442400 | tf_op jit(solution)/shard_map/ppermute | solution.py:292
  31.6 25.7 %exchange.1 = bf16[6912,128]{1,0:T(8,128)(2,1)S(1)} custom-call(bf16[1728,128]{1,0:T(8,128)(2,1)S(1)} %pad_maximum_fusion.q0, bf16[1728,128]{1,0:T(8,128)(2,1)S(1)} %collective-permute-done.7.q1, bf16[1728,128]{1,0:T(8,128)(2,1)S(1)} %collective-permute-done.8.q2, bf16[1728,128]{1,0:T(8,128)(2,1)S(1)} %collective-permute-done.9.q3, ...), custom_call_target="tpu_custom_call" | custom-call | tf_op jit(solution)/shard_map/exchange/pallas_call | solution.py:295
  57.3 25.2 %all_to_all.5.parts = bf16[16,432,128]{2,1,0:T(8,128)(2,1)S(1)} all-to-all(bf16[16,432,128]{2,1,0:T(8,128)(2,1)S(1)} %bitcast.17), channel_id=1, replica_groups=mesh['row'=8,'col'=16] {'col'}, dimensions={0} | all-to-all | bytes 3538944 | tf_op jit(solution)/shard_map/all_to_all | solution.py:311
  82.5 1.2 place.1
  83.7 5.9 %collective-permute-start.10 = (f32[4,192,96]{2,1,0:T(8,128)S(1)}, f32[4,192,96]{2,1,0:T(8,128)S(1)}, u32[]{:S(2)}, u32[]{:S(2)}) collective-permute-start(f32[4,192,96]{2,1,0:T(8,128)S(1)} %get-tuple-element.8), channel_id=1, source_target_pairs={{0,16},{16,0},{32,48},{48,32},{64,80},{80,64},{96,112},{112,96},{1... | collective-permute-start | bytes 884744 | tf_op jit(solution)/shard_map/ppermute | solution.py:325
  89.5 1.3 %collective-permute-done.10 = f32[4,192,96]{2,1,0:T(8,128)S(1)} collective-permute-done((f32[4,192,96]{2,1,0:T(8,128)S(1)}, f32[4,192,96]{2,1,0:T(8,128)S(1)}, u32[]{:S(2)}, u32[]{:S(2)}) %collective-permute-start.10) | collective-permute-done | bytes 294944 | tf_op jit(solution)/shard_map/ppermute | solution.py:325
  91.0 1.8 %collective-permute-start.11 = (f32[192,96]{1,0:T(8,128)S(1)}, f32[192,96]{1,0:T(8,128)S(1)}, u32[]{:S(2)}, u32[]{:S(2)}) collective-permute-start(f32[192,96]{1,0:T(8,128)S(1)} %get-tuple-element.9), channel_id=1, source_target_pairs={{0,64},{16,80},{32,96},{48,112},{64,0},{80,16},{96,32},{112,48},{1... | collective-permute-start | bytes 221192 | tf_op jit(solution)/shard_map/ppermute | solution.py:328
  92.8 1.4 %collective-permute-start.12 = (f32[192,96]{1,0:T(8,128)S(1)}, f32[192,96]{1,0:T(8,128)S(1)}, u32[]{:S(2)}, u32[]{:S(2)}) collective-permute-start(f32[192,96]{1,0:T(8,128)S(1)} %get-tuple-element.11), channel_id=1, source_target_pairs={{0,32},{16,48},{32,64},{48,80},{64,96},{80,112},{96,0},{112,16},{1... | collective-permute-start | bytes 221192 | tf_op jit(solution)/shard_map/ppermute | solution.py:328
  94.2 1.2 %collective-permute-start.13 = (f32[192,96]{1,0:T(8,128)S(1)}, f32[192,96]{1,0:T(8,128)S(1)}, u32[]{:S(2)}, u32[]{:S(2)}) collective-permute-start(f32[192,96]{1,0:T(8,128)S(1)} %get-tuple-element.10), channel_id=1, source_target_pairs={{0,96},{16,112},{32,0},{48,16},{64,32},{80,48},{96,64},{112,80},{1... | collective-permute-start | bytes 221192 | tf_op jit(solution)/shard_map/ppermute | solution.py:328
  95.4 1.1 collective-permute-done.11
  96.6 2.5 %collective-permute-done.12 = f32[192,96]{1,0:T(8,128)S(1)} collective-permute-done((f32[192,96]{1,0:T(8,128)S(1)}, f32[192,96]{1,0:T(8,128)S(1)}, u32[]{:S(2)}, u32[]{:S(2)}) %collective-permute-start.12) | collective-permute-done | bytes 73760 | tf_op jit(solution)/shard_map/ppermute | solution.py:328
  99.1 7.5 %collective-permute-start.14 = (f32[96,96]{1,0:T(8,128)S(1)}, f32[96,96]{1,0:T(8,128)S(1)}, u32[]{:S(2)}, u32[]{:S(2)}) collective-permute-start(f32[96,96]{1,0:T(8,128)S(1)} %get-tuple-element.13), channel_id=1, source_target_pairs={{0,0},{1,1},{2,16},{3,17},{4,32},{5,33},{6,48},{7,49},{8,64},{9,65... | collective-permute-start | bytes 110600 | tf_op jit(solution)/shard_map/ppermute | solution.py:334
  106.6 2.4 %collective-permute-start.15 = (f32[96,96]{1,0:T(8,128)S(1)}, f32[96,96]{1,0:T(8,128)S(1)}, u32[]{:S(2)}, u32[]{:S(2)}) collective-permute-start(f32[96,96]{1,0:T(8,128)S(1)} %get-tuple-element.12), channel_id=1, source_target_pairs={{0,1},{1,0},{2,17},{3,16},{4,33},{5,32},{6,49},{7,48},{8,65},{9,64... | collective-permute-start | bytes 110600 | tf_op jit(solution)/shard_map/ppermute | solution.py:335
  109.0 2.3 %collective-permute-done.14.first = f32[96,96]{1,0:T(8,128)S(1)} collective-permute-done((f32[96,96]{1,0:T(8,128)S(1)}, f32[96,96]{1,0:T(8,128)S(1)}, u32[]{:S(2)}, u32[]{:S(2)}) %collective-permute-start.14) | collective-permute-done | bytes 36896 | tf_op jit(solution)/shard_map/ppermute | solution.py:334
  111.3 5.1 %collective-permute-done.15.second = f32[96,96]{1,0:T(8,128)S(1)} collective-permute-done((f32[96,96]{1,0:T(8,128)S(1)}, f32[96,96]{1,0:T(8,128)S(1)}, u32[]{:S(2)}, u32[]{:S(2)}) %collective-permute-start.15) | collective-permute-done | bytes 36896 | tf_op jit(solution)/shard_map/ppermute | solution.py:335
  (21 shorter events, 6.8 us)
Async XLA Ops:
  0.0 1.8 %collective-permute-start = (bf16[192,96]{1,0:T(8,128)(2,1)}, bf16[192,96]{1,0:T(8,128)(2,1)S(1)}, u32[]{:S(2)}, u32[]{:S(2)}) collective-permute-start(bf16[192,96]{1,0:T(8,128)(2,1)} %param.5), channel_id=1, source_target_pairs={{0,16},{16,0},{32,48},{48,32},{64,80},{80,64},{96,112},{112,96},{1... | collective-permute-start | bytes 110600 | tf_op jit(solution)/shard_map/ppermute | solution.py:259
  1.8 6.4 %collective-permute-start.1 = (bf16[384,96]{1,0:T(8,128)(2,1)S(1)}, bf16[384,96]{1,0:T(8,128)(2,1)S(1)}, u32[]{:S(2)}, u32[]{:S(2)}) collective-permute-start(bf16[384,96]{1,0:T(8,128)(2,1)S(1)} %constant_dynamic-update-slice_fusion.p0), channel_id=1, source_target_pairs={{0,64},{16,80},{32,96},{48,112},{64,0},{80,16},{96,32},{112,48},{1... | collective-permute-start | bytes 221192 | tf_op jit(solution)/shard_map/ppermute | solution.py:260
  4.8 4.7 %collective-permute-start.2 = (bf16[384,96]{1,0:T(8,128)(2,1)S(1)}, bf16[384,96]{1,0:T(8,128)(2,1)S(1)}, u32[]{:S(2)}, u32[]{:S(2)}) collective-permute-start(bf16[384,96]{1,0:T(8,128)(2,1)S(1)} %constant_dynamic-update-slice_fusion.p0), channel_id=1, source_target_pairs={{0,32},{16,48},{32,64},{48,80},{64,96},{80,112},{96,0},{112,16},{1... | collective-permute-start | bytes 221192 | tf_op jit(solution)/shard_map/ppermute | solution.py:260
  5.2 4.7 %collective-permute-start.3 = (bf16[384,96]{1,0:T(8,128)(2,1)S(1)}, bf16[384,96]{1,0:T(8,128)(2,1)S(1)}, u32[]{:S(2)}, u32[]{:S(2)}) collective-permute-start(bf16[384,96]{1,0:T(8,128)(2,1)S(1)} %constant_dynamic-update-slice_fusion.p0), channel_id=1, source_target_pairs={{0,96},{16,112},{32,0},{48,16},{64,32},{80,48},{96,64},{112,80},{1... | collective-permute-start | bytes 221192 | tf_op jit(solution)/shard_map/ppermute | solution.py:260
  11.3 5.3 %collective-permute-start.4 = (bf16[432,128]{1,0:T(8,128)(2,1)S(1)}, bf16[432,128]{1,0:T(8,128)(2,1)S(1)}, u32[]{:S(2)}, u32[]{:S(2)}) collective-permute-start(bf16[432,128]{1,0:T(8,128)(2,1)S(1)} %select.3), channel_id=1, source_target_pairs={{0,2},{1,3},{2,0},{3,1},{4,6},{5,7},{6,4},{7,5},{8,10},{9,11},{10,... | collective-permute-start | bytes 331784 | tf_op jit(solution)/shard_map/ppermute | solution.py:290
  11.4 6.1 %collective-permute-start.5 = (bf16[432,128]{1,0:T(8,128)(2,1)S(1)}, bf16[432,128]{1,0:T(8,128)(2,1)S(1)}, u32[]{:S(2)}, u32[]{:S(2)}) collective-permute-start(bf16[432,128]{1,0:T(8,128)(2,1)S(1)} %select.3), channel_id=1, source_target_pairs={{0,1},{1,2},{2,3},{3,0},{4,5},{5,6},{6,7},{7,4},{8,9},{9,10},{10,1... | collective-permute-start | bytes 331784 | tf_op jit(solution)/shard_map/ppermute | solution.py:290
  13.0 4.7 %collective-permute-start.6 = (bf16[432,128]{1,0:T(8,128)(2,1)S(1)}, bf16[432,128]{1,0:T(8,128)(2,1)S(1)}, u32[]{:S(2)}, u32[]{:S(2)}) collective-permute-start(bf16[432,128]{1,0:T(8,128)(2,1)S(1)} %select.3), channel_id=1, source_target_pairs={{0,3},{1,0},{2,1},{3,2},{4,7},{5,4},{6,5},{7,6},{8,11},{9,8},{10,9... | collective-permute-start | bytes 331784 | tf_op jit(solution)/shard_map/ppermute | solution.py:290
  17.7 8.8 %collective-permute-start.7 = (bf16[1728,128]{1,0:T(8,128)(2,1)S(1)}, bf16[1728,128]{1,0:T(8,128)(2,1)S(1)}, u32[]{:S(2)}, u32[]{:S(2)}) collective-permute-start(bf16[1728,128]{1,0:T(8,128)(2,1)S(1)} %pad_maximum_fusion.q0), channel_id=1, source_target_pairs={{0,8},{1,9},{2,10},{3,11},{4,12},{5,13},{6,14},{7,15},{8,0},{9,1},... | collective-permute-start | bytes 1327112 | tf_op jit(solution)/shard_map/ppermute | solution.py:292
  20.6 10.8 %collective-permute-start.8 = (bf16[1728,128]{1,0:T(8,128)(2,1)S(1)}, bf16[1728,128]{1,0:T(8,128)(2,1)S(1)}, u32[]{:S(2)}, u32[]{:S(2)}) collective-permute-start(bf16[1728,128]{1,0:T(8,128)(2,1)S(1)} %pad_maximum_fusion.q0), channel_id=1, source_target_pairs={{0,4},{1,5},{2,6},{3,7},{4,8},{5,9},{6,10},{7,11},{8,12},{9,13},{1... | collective-permute-start | bytes 1327112 | tf_op jit(solution)/shard_map/ppermute | solution.py:292
  20.9 10.8 %collective-permute-start.9 = (bf16[1728,128]{1,0:T(8,128)(2,1)S(1)}, bf16[1728,128]{1,0:T(8,128)(2,1)S(1)}, u32[]{:S(2)}, u32[]{:S(2)}) collective-permute-start(bf16[1728,128]{1,0:T(8,128)(2,1)S(1)} %pad_maximum_fusion.q0), channel_id=1, source_target_pairs={{0,12},{1,13},{2,14},{3,15},{4,0},{5,1},{6,2},{7,3},{8,4},{9,5},{1... | collective-permute-start | bytes 1327112 | tf_op jit(solution)/shard_map/ppermute | solution.py:292
  83.7 7.2 %collective-permute-start.10 = (f32[4,192,96]{2,1,0:T(8,128)S(1)}, f32[4,192,96]{2,1,0:T(8,128)S(1)}, u32[]{:S(2)}, u32[]{:S(2)}) collective-permute-start(f32[4,192,96]{2,1,0:T(8,128)S(1)} %get-tuple-element.8), channel_id=1, source_target_pairs={{0,16},{16,0},{32,48},{48,32},{64,80},{80,64},{96,112},{112,96},{1... | collective-permute-start | bytes 884744 | tf_op jit(solution)/shard_map/ppermute | solution.py:325
  91.0 5.6 %collective-permute-start.11 = (f32[192,96]{1,0:T(8,128)S(1)}, f32[192,96]{1,0:T(8,128)S(1)}, u32[]{:S(2)}, u32[]{:S(2)}) collective-permute-start(f32[192,96]{1,0:T(8,128)S(1)} %get-tuple-element.9), channel_id=1, source_target_pairs={{0,64},{16,80},{32,96},{48,112},{64,0},{80,16},{96,32},{112,48},{1... | collective-permute-start | bytes 221192 | tf_op jit(solution)/shard_map/ppermute | solution.py:328
  92.8 6.3 %collective-permute-start.12 = (f32[192,96]{1,0:T(8,128)S(1)}, f32[192,96]{1,0:T(8,128)S(1)}, u32[]{:S(2)}, u32[]{:S(2)}) collective-permute-start(f32[192,96]{1,0:T(8,128)S(1)} %get-tuple-element.11), channel_id=1, source_target_pairs={{0,32},{16,48},{32,64},{48,80},{64,96},{80,112},{96,0},{112,16},{1... | collective-permute-start | bytes 221192 | tf_op jit(solution)/shard_map/ppermute | solution.py:328
  94.2 4.8 %collective-permute-start.13 = (f32[192,96]{1,0:T(8,128)S(1)}, f32[192,96]{1,0:T(8,128)S(1)}, u32[]{:S(2)}, u32[]{:S(2)}) collective-permute-start(f32[192,96]{1,0:T(8,128)S(1)} %get-tuple-element.10), channel_id=1, source_target_pairs={{0,96},{16,112},{32,0},{48,16},{64,32},{80,48},{96,64},{112,80},{1... | collective-permute-start | bytes 221192 | tf_op jit(solution)/shard_map/ppermute | solution.py:328
  99.1 12.2 %collective-permute-start.14 = (f32[96,96]{1,0:T(8,128)S(1)}, f32[96,96]{1,0:T(8,128)S(1)}, u32[]{:S(2)}, u32[]{:S(2)}) collective-permute-start(f32[96,96]{1,0:T(8,128)S(1)} %get-tuple-element.13), channel_id=1, source_target_pairs={{0,0},{1,1},{2,16},{3,17},{4,32},{5,33},{6,48},{7,49},{8,64},{9,65... | collective-permute-start | bytes 110600 | tf_op jit(solution)/shard_map/ppermute | solution.py:334
  106.6 9.9 %collective-permute-start.15 = (f32[96,96]{1,0:T(8,128)S(1)}, f32[96,96]{1,0:T(8,128)S(1)}, u32[]{:S(2)}, u32[]{:S(2)}) collective-permute-start(f32[96,96]{1,0:T(8,128)S(1)} %get-tuple-element.12), channel_id=1, source_target_pairs={{0,1},{1,0},{2,17},{3,16},{4,33},{5,32},{6,49},{7,48},{8,65},{9,64... | collective-permute-start | bytes 110600 | tf_op jit(solution)/shard_map/ppermute | solution.py:335
